TPU v7x, 32 devices: a whole 2x2x4 slice. The times are simulated.
32 devices in a mesh: wide: 8 (over y, x, core), narrow: 4 (over z).
Axes of the slice: x: 2, y: 2, z: 4, core: 2. Of those that a mesh axis runs over, the one named last changes fastest.
Arguments:
- inputs: bfloat16 [64, 1024, 512], P('wide', 'narrow'), may hold values from -6 to 6
- positions: int32 [64, 1024], P('wide'), may hold values from 0 to 1023, as said below
- members_index: int32 [1024, 2, 56], P('narrow'), may hold values from 0 to 63, as said below
- members_mask: int32 [1024, 2, 56], P('narrow'), may hold values from 0 to 1, as said below
- gain_attn: float32 [512], replicated, may hold values from 0.5 to 1.5
- input_projection_weight: bfloat16 [512, 3, 512], P(None, None, 'narrow'), may hold values from -0.25 to 0.25
- output_projection_weight: bfloat16 [512, 512], P('narrow'), may hold values from -2 to 2
- gain_mixer: float32 [512], replicated, may hold values from 0.5 to 1.5
- weight_router: bfloat16 [512, 8], replicated, may hold values from -0.1875 to 0.1875
- weight_up: bfloat16 [8, 512, 2048], P(None, None, 'narrow'), may hold values from -1 to 1
- weight_down: bfloat16 [8, 2048, 512], P(None, 'narrow'), may hold values from -3 to 3
- cotangent: bfloat16 [64, 1024, 512], P('wide', 'narrow'), may hold values from -6 to 6
Outputs:
- outputs: bfloat16 [64, 1024, 512], P('wide', 'narrow')
- grad_inputs: float32 [64, 1024, 512], P('wide', 'narrow')
- grad_gain_attn: float32 [512], replicated
- grad_inproj: float32 [512, 3, 512], P(None, None, 'narrow')
- grad_outproj: float32 [512, 512], P('narrow')
- grad_gain_mixer: float32 [512], replicated
- grad_router: float32 [512, 8], replicated
- grad_up: float32 [8, 512, 2048], P(None, None, 'narrow')
- grad_down: float32 [8, 2048, 512], P(None, 'narrow')
Inputs may be any that keep to these rules, and one draw needn't show every extreme that they name: `positions`: 0 at a document's first token and one more at each next token; in each block of 8 sequences in a row one sequence, drawn from the seed, holds exactly two documents, the second of which begins between token 896 and token 1023. `members_index`: at each position the live slots of its 2 groups name every sequence exactly once. `members_mask`: each group's row is 1 on its first 8 to 56 slots and 0 after; at each position one group has all 56 slots live.
All inputs are finite; a program needn't handle non-finite values.
Results may differ from a plain program's by a relative error of at most 0.034.
Values may be sent and summed in bfloat16 or wider, within the bound.
A program may use at most 320 MiB of HBM per device.

v0:
```python
import jax
import jax.numpy as jnp
from jax import lax
from jax.sharding import PartitionSpec as P

HEAD_DIM = 64


epsilon = 1e-06
highest = lax.Precision.HIGHEST


def normalize(values, gain):
    scaling = lax.rsqrt(jnp.mean(values * values, axis=-1, keepdims=True) + epsilon)
    unit_rows = values * scaling
    return (unit_rows * gain, unit_rows, scaling)


def norm_back(grad_rows, unit_rows, scaling, gain):
    gain_grad = jnp.sum(grad_rows * unit_rows, axis=tuple(range(grad_rows.ndim - 1)))
    grad_unit = grad_rows * gain
    grad_values = scaling * (
        grad_unit - unit_rows * jnp.mean(grad_unit * unit_rows, axis=-1, keepdims=True)
    )
    return (grad_values, gain_grad)


def expert_back(mixed_rows, grad_rows, weight_up, weight_down):
    pre_act = jnp.einsum("ged,edf->gef", mixed_rows, weight_up, preferred_element_type=jnp.float32)
    act_full, gelu_back = jax.vjp(jax.nn.gelu, pre_act)
    grad_act = jnp.einsum(
        "ged,efd->gef", grad_rows, weight_down, preferred_element_type=jnp.float32
    )
    grad_pre = gelu_back(grad_act)[0].astype(jnp.bfloat16)
    return (act_full.astype(jnp.bfloat16), grad_pre)


def per_device(
    inputs,
    positions,
    members_index,
    members_mask,
    gain_attn,
    input_projection_weight,
    output_projection_weight,
    gain_mixer,
    weight_router,
    weight_up,
    weight_down,
    cotangent,
):
    seq_dev, local_len, features = inputs.shape
    seq_len = positions.shape[1]
    group_count = members_index.shape[1]
    slot_count = members_index.shape[2]
    wide_count = lax.axis_size("wide")
    pos_dev = local_len // wide_count
    group_rows = pos_dev * group_count
    seq_total = seq_dev * wide_count
    head_feat = input_projection_weight.shape[2]
    heads_local = head_feat // HEAD_DIM
    scaling_attn = HEAD_DIM ** (-0.5)
    block_rows = min(512, seq_len)
    residual = inputs.astype(jnp.float32)
    normed_one, unit_one, scale_one = normalize(residual, gain_attn)
    collected_rows = lax.all_gather(normed_one.astype(jnp.bfloat16), "narrow", axis=1, tiled=True)
    projected = jnp.einsum(
        "aoe,epi->aopi", collected_rows, input_projection_weight, preferred_element_type=jnp.float32
    ).astype(jnp.bfloat16)
    queries = projected[:, :, 0].reshape(seq_dev, seq_len, heads_local, HEAD_DIM)
    keys_local = projected[:, :, 1].reshape(seq_dev, seq_len, heads_local, HEAD_DIM)
    values_local = projected[:, :, 2].reshape(seq_dev, seq_len, heads_local, HEAD_DIM)
    key_order = jnp.arange(seq_len, dtype=jnp.int32)

    def scores_of(first_row):
        query_block = queries[:, first_row : first_row + block_rows]
        raw_scores = (
            jnp.einsum(
                "sqhd,skhd->shqk", query_block, keys_local, preferred_element_type=jnp.float32
            )
            * scaling_attn
        )
        row_index = first_row + jnp.arange(block_rows, dtype=jnp.int32)
        distance = row_index[:, None] - key_order[None, :]
        position_rows = positions[:, first_row : first_row + block_rows]
        allowed = (distance >= 0)[None] & (distance[None] <= position_rows[:, :, None])
        return (jnp.where(allowed[:, None], raw_scores, -1e30), query_block)

    attended_list = []
    logsum_list = []
    for first_row in range(0, seq_len, block_rows):
        logits, query_block = scores_of(first_row)
        highest_score = jnp.max(logits, axis=-1, keepdims=True)
        exponent = jnp.exp(logits - highest_score)
        denominator = jnp.sum(exponent, axis=-1, keepdims=True)
        probabilities = (exponent / denominator).astype(jnp.bfloat16)
        attended_list.append(
            jnp.einsum(
                "shqk,skhd->qshd", probabilities, values_local, preferred_element_type=jnp.float32
            ).astype(jnp.bfloat16)
        )
        logsum_list.append(highest_score + jnp.log(denominator))
    attention_result = jnp.concatenate(attended_list, axis=0).reshape(seq_len, seq_dev, head_feat)
    current_row_block = attention_result
    attn_sum = lax.psum_scatter(
        jnp.einsum(
            "pbi,iq->pbq",
            current_row_block,
            output_projection_weight,
            preferred_element_type=jnp.float32,
        ).astype(jnp.bfloat16),
        "narrow",
        scatter_dimension=0,
        tiled=True,
    ).astype(jnp.float32)
    hidden_one = residual + jnp.transpose(attn_sum, (1, 0, 2))
    normed_two, unit_two, scale_two = normalize(hidden_one, gain_mixer)
    grouped, grads_grouped = (
        lax.all_to_all(
            normed_two.astype(jnp.bfloat16), "wide", split_axis=1, concat_axis=0, tiled=True
        ),
        lax.all_to_all(cotangent, "wide", split_axis=1, concat_axis=0, tiled=True),
    )
    offset_rows = lax.axis_index("wide") * pos_dev
    index_rows = lax.dynamic_slice_in_dim(members_index, offset_rows, pos_dev, 0)
    live_full = lax.dynamic_slice_in_dim(members_mask, offset_rows, pos_dev, 0) > 0
    selector = (
        (index_rows[..., None] == jnp.arange(seq_total, dtype=jnp.int32)[None, None, None, :])
        & live_full[..., None]
    ).astype(jnp.bfloat16)
    live_slots = live_full.reshape(group_rows, slot_count)
    members = jnp.einsum(
        "pgjs,spd->pgjd", selector, grouped, preferred_element_type=jnp.float32
    ).astype(jnp.bfloat16)
    members = members.reshape(group_rows, slot_count, features)
    router_logits = jnp.einsum(
        "pjd,de->pje", members, weight_router, preferred_element_type=jnp.float32
    )
    router_logits = jnp.where(live_slots[:, :, None], router_logits, -1e30)
    router_peak = jnp.max(router_logits, axis=1, keepdims=True)
    router_exp = jnp.exp(router_logits - router_peak)
    weights = router_exp / jnp.sum(router_exp, axis=1, keepdims=True)
    weights_low = weights.astype(jnp.bfloat16)
    weights_wide = weights_low.astype(jnp.float32)
    mixed_tokens = jnp.einsum(
        "pje,pjd->ped", weights_low, members, preferred_element_type=jnp.float32
    ).astype(jnp.bfloat16)
    all_mixed = lax.all_gather(mixed_tokens, "narrow", axis=0, tiled=True)
    current_row_block = all_mixed
    pre_act = jnp.einsum(
        "ged,edf->gef", current_row_block, weight_up, preferred_element_type=jnp.float32
    )
    act_low = jax.nn.gelu(pre_act).astype(jnp.bfloat16)
    expert_out = lax.psum_scatter(
        jnp.einsum("gef,efd->ged", act_low, weight_down, preferred_element_type=jnp.float32).astype(
            jnp.bfloat16
        ),
        "narrow",
        scatter_dimension=0,
        tiled=True,
    ).astype(jnp.float32)
    member_out = jnp.einsum("pje,ped->pjd", weights_wide, expert_out, precision=highest).astype(
        jnp.bfloat16
    )
    member_out = member_out.reshape(pos_dev, group_count, slot_count, features)
    token_out = jnp.einsum(
        "pgjs,pgjd->spd", selector, member_out, preferred_element_type=jnp.float32
    ).astype(jnp.bfloat16)
    grad_member_out = jnp.einsum(
        "pgjs,spd->pgjd", selector, grads_grouped, preferred_element_type=jnp.float32
    )
    grad_member_out = grad_member_out.reshape(group_rows, slot_count, features)
    grad_expert = jnp.einsum(
        "pje,pjd->ped", weights_wide, grad_member_out, precision=highest
    ).astype(jnp.bfloat16)
    grad_weights = jnp.einsum("pjd,ped->pje", grad_member_out, expert_out, precision=highest)
    all_grad = lax.all_gather(grad_expert, "narrow", axis=0, tiled=True)
    act_local, grad_pre = expert_back(all_mixed, all_grad, weight_up, weight_down)

    def mixed_rows(first_row, row_count):
        return jnp.einsum("gef,edf->ged", grad_pre, weight_up, preferred_element_type=jnp.float32)

    grad_mixed = lax.psum_scatter(
        mixed_rows(jnp.int32(0), group_rows * lax.axis_size("narrow")).astype(jnp.bfloat16),
        "narrow",
        scatter_dimension=0,
        tiled=True,
    )
    grad_weights = grad_weights + jnp.einsum(
        "ped,pjd->pje", grad_mixed, members, preferred_element_type=jnp.float32
    )
    inner_sum = jnp.sum(weights * grad_weights, axis=1, keepdims=True)
    grad_logits = (weights * (grad_weights - inner_sum)).astype(jnp.bfloat16)
    grad_members = jnp.einsum(
        "pje,ped->pjd", weights_low, grad_mixed, preferred_element_type=jnp.float32
    )
    grad_members = grad_members + jnp.einsum(
        "pje,de->pjd", grad_logits, weight_router, preferred_element_type=jnp.float32
    )
    router_grad = jnp.einsum(
        "pjd,pje->de", members, grad_logits, preferred_element_type=jnp.float32
    )
    grad_members = grad_members.reshape(pos_dev, group_count, slot_count, features)
    grad_grouped = jnp.einsum(
        "pgjs,pgjd->spd", selector.astype(jnp.float32), grad_members, precision=highest
    ).astype(jnp.bfloat16)
    mixer_out, grad_normed_two = (
        lax.all_to_all(token_out, "wide", split_axis=0, concat_axis=1, tiled=True),
        lax.all_to_all(grad_grouped, "wide", split_axis=0, concat_axis=1, tiled=True),
    )
    outputs = (hidden_one + mixer_out.astype(jnp.float32)).astype(jnp.bfloat16)
    grad_hidden_part, gain_two_grad = norm_back(
        grad_normed_two.astype(jnp.float32), unit_two, scale_two, gain_mixer
    )
    grad_hidden = cotangent.astype(jnp.float32) + grad_hidden_part
    complete_gradient = lax.all_gather(
        grad_hidden.astype(jnp.bfloat16), "narrow", axis=1, tiled=True
    )
    outproj_grad = jnp.einsum(
        "hzp,zhi->pi", attention_result, complete_gradient, preferred_element_type=jnp.float32
    )
    grad_attended = jnp.einsum(
        "igv,jv->gij",
        complete_gradient,
        output_projection_weight,
        preferred_element_type=jnp.float32,
    ).astype(jnp.bfloat16)
    grad_attended = grad_attended.reshape(seq_len, seq_dev, heads_local, HEAD_DIM)
    grad_query_list = []
    grad_keys = jnp.zeros((seq_dev, seq_len, heads_local, HEAD_DIM), jnp.float32)
    grad_values = jnp.zeros((seq_dev, seq_len, heads_local, HEAD_DIM), jnp.float32)
    for block_number, first_row in enumerate(range(0, seq_len, block_rows)):
        logits, query_block = scores_of(first_row)
        probabilities = jnp.exp(logits - logsum_list[block_number])
        grad_out_block = grad_attended[first_row : first_row + block_rows]
        grad_probs = jnp.einsum(
            "qshd,skhd->shqk", grad_out_block, values_local, preferred_element_type=jnp.float32
        )
        grad_values = grad_values + jnp.einsum(
            "shqk,qshd->skhd",
            probabilities.astype(jnp.bfloat16),
            grad_out_block,
            preferred_element_type=jnp.float32,
        )
        row_inner = jnp.sum(probabilities * grad_probs, axis=-1, keepdims=True)
        grad_scores = (probabilities * (grad_probs - row_inner)).astype(jnp.bfloat16)
        grad_query_list.append(
            jnp.einsum(
                "shqk,skhd->sqhd", grad_scores, keys_local, preferred_element_type=jnp.float32
            )
            * scaling_attn
        )
        grad_keys = (
            grad_keys
            + jnp.einsum(
                "shqk,sqhd->skhd", grad_scores, query_block, preferred_element_type=jnp.float32
            )
            * scaling_attn
        )
    grad_queries = jnp.concatenate(grad_query_list, axis=1)
    projection_gradient = (
        jnp.stack([grad_queries, grad_keys, grad_values], axis=2)
        .reshape(seq_dev, seq_len, 3, head_feat)
        .astype(jnp.bfloat16)
    )
    inproj_grad = jnp.einsum(
        "qto,qtnr->onr", collected_rows, projection_gradient, preferred_element_type=jnp.float32
    )
    current_row_block = projection_gradient
    grad_normed_one = lax.psum_scatter(
        jnp.einsum(
            "slcf,dcf->lsd",
            current_row_block,
            input_projection_weight,
            preferred_element_type=jnp.float32,
        ).astype(jnp.bfloat16),
        "narrow",
        scatter_dimension=0,
        tiled=True,
    ).astype(jnp.float32)
    grad_normed_one = (
        jnp.transpose(grad_normed_one, (1, 0, 2)).astype(jnp.bfloat16).astype(jnp.float32)
    )
    grad_input_part, gain_one_grad = norm_back(grad_normed_one, unit_one, scale_one, gain_attn)
    grad_inputs = grad_hidden + grad_input_part
    up_grad = jnp.einsum("ged,gef->edf", all_mixed, grad_pre, preferred_element_type=jnp.float32)
    down_grad = jnp.einsum("gef,ged->efd", act_local, all_grad, preferred_element_type=jnp.float32)
    inproj_grad, outproj_grad, up_grad, down_grad = (
        lax.psum(inproj_grad.astype(jnp.bfloat16), "wide").astype(jnp.float32),
        lax.psum(outproj_grad.astype(jnp.bfloat16), "wide").astype(jnp.float32),
        lax.psum(up_grad.astype(jnp.bfloat16), "wide").astype(jnp.float32),
        lax.psum(down_grad.astype(jnp.bfloat16), "wide").astype(jnp.float32),
    )
    gain_one_grad, gain_two_grad, router_grad = lax.psum(
        (gain_one_grad, gain_two_grad, router_grad), ("wide", "narrow")
    )
    return (
        outputs,
        grad_inputs,
        gain_one_grad,
        inproj_grad,
        outproj_grad,
        gain_two_grad,
        router_grad,
        up_grad,
        down_grad,
    )


def solution(mesh):
    in_specs = (
        P("wide", "narrow", None),
        P("wide", None),
        P("narrow", None, None),
        P("narrow", None, None),
        P(),
        P(None, None, "narrow"),
        P("narrow", None),
        P(),
        P(),
        P(None, None, "narrow"),
        P(None, "narrow", None),
        P("wide", "narrow", None),
    )
    out_specs = (
        P("wide", "narrow", None),
        P("wide", "narrow", None),
        P(),
        P(None, None, "narrow"),
        P("narrow", None),
        P(),
        P(),
        P(None, None, "narrow"),
        P(None, "narrow", None),
    )
    return jax.shard_map(
        per_device, mesh=mesh, in_specs=in_specs, out_specs=out_specs, check_vma=False
    )
```

profile of v0, /device:TPU:3, one launch (start us, length us, event | category | flops | bytes accessed | tf_op | source)
XLA Modules:
  0.0 1417.2 jit_solution(11856697867752616200)
XLA Ops:
  21.8 142.8 %all-gather.5.cloned.1.call-done = bf16[8,1024,512]{2,1,0:T(8,128)(2,1)} async-done(((bf16[8,256,512]{2,1,0:T(8,128)(2,1)}), bf16[8,1024,512]{2,1,0:T(8,128)(2,1)}) %all-gather.5.cloned.1.call-update) | async-done | bytes 8388624 | tf_op jit(solution)/shard_map/all_gather | solution.py:66
  174.3 17.5 %fusion.118 = (f32[8,2,512]{2,1,0:T(2,128)S(1)}, f32[8,2,512,1024]{3,2,1,0:T(8,128)}) fusion(bf16[8,1024,2,64]{1,3,2,0:T(8,128)(2,1)S(1)} %bitcast.251, bf16[8,1024,2,64]{1,3,2,0:T(8,128)(2,1)} %bitcast.269, pred[8,512,1024]{2,1,0:T(8,128)(4,1)} %get-tuple-element.41), kind=kOutput, calls=%fused_computation.171 | convolution fusion | flops 1098899456 | bytes 40927232 | tf_op jit(solution)/shard_map/sqhd,skhd->shqk/dot_general | solution.py:78
  191.8 17.1 %fusion.119 = (f32[8,2,512]{2,1,0:T(2,128)S(1)}, f32[8,2,512,1024]{3,2,1,0:T(8,128)}) fusion(bf16[8,1024,2,64]{1,3,2,0:T(8,128)(2,1)S(1)} %bitcast.252, bf16[8,1024,2,64]{1,3,2,0:T(8,128)(2,1)} %bitcast.270, pred[8,512,1024]{2,1,0:T(8,128)(4,1)} %get-tuple-element.42), kind=kOutput, calls=%fused_computation.172 | convolution fusion | flops 1098899456 | bytes 40927232 | tf_op jit(solution)/shard_map/sqhd,skhd->shqk/dot_general | solution.py:78
  208.9 14.4 %fusion.2 = f32[8,2,512]{2,1,0:T(2,128)S(1)} fusion(f32[8,2,512,1024]{3,2,1,0:T(8,128)} %get-tuple-element.30, f32[8,2,512]{2,1,0:T(2,128)S(1)} %get-tuple-element.29), kind=kLoop, calls=%fused_computation.14 | loop fusion | flops 16769024 | bytes 33619968 | tf_op jit(solution)/shard_map/reduce_sum | solution.py:95
  236.2 14.2 %fusion.1 = f32[8,2,512]{2,1,0:T(2,128)S(1)} fusion(f32[8,2,512,1024]{3,2,1,0:T(8,128)} %get-tuple-element.32, f32[8,2,512]{2,1,0:T(2,128)S(1)} %get-tuple-element.31), kind=kLoop, calls=%fused_computation.13 | loop fusion | flops 16769024 | bytes 33619968 | tf_op jit(solution)/shard_map/reduce_sum | solution.py:95
  250.4 13.4 fusion.71
  271.2 142.4 %reduce-scatter.5.cloned.1.call-done = bf16[256,8,512]{2,0,1:T(8,128)(2,1)} async-done(((bf16[1024,8,512]{2,0,1:T(8,128)(2,1)}), bf16[256,8,512]{2,0,1:T(8,128)(2,1)}) %reduce-scatter.5.cloned.1.call-update) | async-done | bytes 2097168 | tf_op jit(solution)/shard_map/reduce_scatter | solution.py:105
  425.2 24.7 %all-to-all-done = bf16[8,256,512]{2,0,1:T(8,128)(2,1)} async-done(((bf16[8,256,512]{2,0,1:T(8,128)(2,1)}), bf16[8,256,512]{2,0,1:T(8,128)(2,1)}, u32[]{:S(2)}, u32[]{:S(2)}) %all-to-all-start) | async-done | bytes 2097184 | tf_op jit(solution)/shard_map/all_to_all | solution.py:119
  464.3 29.2 %all_to_all.54 = bf16[8,256,512]{2,0,1:T(8,128)(2,1)S(1)} all-to-all(bf16[8,256,512]{2,0,1:T(8,128)(2,1)S(1)} %copy.109), channel_id=1, replica_groups=mesh['wide'=8,'narrow'=4] {'wide'}, dimensions={1} | all-to-all | bytes 4194304 | tf_op jit(solution)/shard_map/all_to_all | solution.py:122
  516.8 37.1 %all-gather.9.cloned.1.call-done = bf16[256,8,512]{2,1,0:T(8,128)(2,1)} async-done(((bf16[64,8,512]{2,1,0:T(8,128)(2,1)}), bf16[256,8,512]{2,1,0:T(8,128)(2,1)}) %all-gather.9.cloned.1.call-update) | async-done | bytes 2097168 | tf_op jit(solution)/shard_map/all_gather | solution.py:177
  566.5 32.1 %reduce-scatter.7.cloned.1.call-done = bf16[64,8,512]{2,0,1:T(8,128)(2,1)} async-done(((bf16[256,8,512]{2,0,1:T(8,128)(2,1)}), bf16[64,8,512]{2,0,1:T(8,128)(2,1)}) %reduce-scatter.7.cloned.1.call-update) | async-done | bytes 524304 | tf_op jit(solution)/shard_map/reduce_scatter | solution.py:154
  605.2 39.4 %reduce-scatter.9.cloned.1.call-done = bf16[64,8,512]{2,0,1:T(8,128)(2,1)} async-done(((bf16[256,8,512]{2,0,1:T(8,128)(2,1)}), bf16[64,8,512]{2,0,1:T(8,128)(2,1)}) %reduce-scatter.9.cloned.1.call-update) | async-done | bytes 524304 | tf_op jit(solution)/shard_map/reduce_scatter | solution.py:183
  656.3 29.4 %all_to_all.55 = bf16[64,32,512]{2,1,0:T(8,128)(2,1)S(1)} all-to-all(bf16[64,32,512]{2,1,0:T(8,128)(2,1)S(1)} %copy.115), channel_id=1, replica_groups=mesh['wide'=8,'narrow'=4] {'wide'}, dimensions={0} | all-to-all | bytes 4194304 | tf_op jit(solution)/shard_map/all_to_all | solution.py:209
  705.3 136.4 %all-gather.11.cloned.1.call-done = bf16[8,1024,512]{2,1,0:T(8,128)(2,1)} async-done(((bf16[8,256,512]{2,1,0:T(8,128)(2,1)}), bf16[8,1024,512]{2,1,0:T(8,128)(2,1)}) %all-gather.11.cloned.1.call-update) | async-done | bytes 8388624 | tf_op jit(solution)/shard_map/all_gather | solution.py:216
  849.8 22.9 %multiply_reduce_fusion.1 = (f32[8,2,512]{2,1,0:T(2,128)}, f32[8,2,512,1024]{3,2,1,0:T(8,128)}) fusion(f32[8,2,512,1024]{3,2,1,0:T(8,128)} %get-tuple-element.32, f32[8,2,512]{2,1,0:T(2,128)S(1)} %bitcast.277, bf16[512,8,2,64]{0,3,2,1:T(8,128)(2,1)S(1)} %bitcast.264, bf16[8,1024,2,64]{1,3,2,0:T(8,128)(2,1)S(1)} %bitcast.260), kind=kOutput, calls=%fused_computation.5 | convolution fusion | flops 1098899456 | bytes 70320128 | tf_op jit(solution)/shard_map/qshd,skhd->shqk/dot_general | solution.py:236
  872.7 28.1 %multiply_convert_fusion.1 = bf16[8,2,512,1024]{3,2,1,0:T(8,128)(2,1)} fusion(f32[8,2,512,1024]{3,2,1,0:T(8,128)} %get-tuple-element.38, f32[8,2,512,1024]{3,2,1,0:T(8,128)} %get-tuple-element.32, f32[8,2,512]{2,1,0:T(2,128)} %get-tuple-element.37, f32[8,2,512]{2,1,0:T(2,128)} %bitcast.278), kind=kLoop, calls=%fused_computation.4 | loop fusion | flops 33554432 | bytes 83951616 | tf_op jit(solution)/shard_map/convert_element_type | solution.py:246
  924.0 15.5 %fusion.5 = f32[8,2,64,1024]{3,2,1,0:T(8,128)} fusion(bf16[512,8,2,64]{0,3,2,1:T(8,128)(2,1)S(1)} %bitcast.266, f32[8,2,512,1024]{3,2,1,0:T(8,128)} %get-tuple-element.30, f32[8,2,512]{2,1,0:T(2,128)} %bitcast.280), kind=kOutput, calls=%fused_computation.17 | convolution fusion | flops 1090519040 | bytes 38830080 | tf_op jit(solution)/shard_map/shqk,qshd->skhd/dot_general | solution.py:239
  939.5 23.0 %multiply_reduce_fusion = (f32[8,2,512]{2,1,0:T(2,128)}, f32[8,2,512,1024]{3,2,1,0:T(8,128)}) fusion(f32[8,2,512,1024]{3,2,1,0:T(8,128)} %get-tuple-element.30, f32[8,2,512]{2,1,0:T(2,128)} %bitcast.281, bf16[512,8,2,64]{0,3,2,1:T(8,128)(2,1)S(1)} %bitcast.267, bf16[8,1024,2,64]{1,3,2,0:T(8,128)(2,1)S(1)} %bitcast.261), kind=kOutput, calls=%fused_computation.2 | convolution fusion | flops 1098899456 | bytes 70320128 | tf_op jit(solution)/shard_map/qshd,skhd->shqk/dot_general | solution.py:236
  962.5 16.4 %add_convert_fusion = bf16[8,2,64,1024]{3,2,1,0:T(8,128)(2,1)} fusion(f32[8,2,64,1024]{3,2,1,0:T(8,128)} %fusion.5, bf16[512,8,2,64]{0,3,2,1:T(8,128)(2,1)S(1)} %bitcast.265, f32[8,2,512,1024]{3,2,1,0:T(8,128)} %get-tuple-element.32, f32[8,2,512]{2,1,0:T(2,128)} %bitcast.279), kind=kOutput, calls=%fused_computation.71 | convolution fusion | flops 1092616192 | bytes 40927232 | tf_op jit(solution)/shard_map/shqk,qshd->skhd/dot_general | solution.py:239
  982.9 27.7 %multiply_convert_fusion = bf16[8,2,512,1024]{3,2,1,0:T(8,128)(2,1)} fusion(f32[8,2,512,1024]{3,2,1,0:T(8,128)} %get-tuple-element.40, f32[8,2,512,1024]{3,2,1,0:T(8,128)} %get-tuple-element.30, f32[8,2,512]{2,1,0:T(2,128)S(1)} %copy-done.41, f32[8,2,512]{2,1,0:T(2,128)S(1)} %bitcast.282), kind=kLoop, calls=%fused_computation.1 | loop fusion | flops 33554432 | bytes 83951616 | tf_op jit(solution)/shard_map/convert_element_type | solution.py:246
  1084.2 35.6 %all-to-all-done.1 = bf16[64,32,512]{2,1,0:T(8,128)(2,1)S(1)} async-done(((bf16[64,32,512]{2,1,0:T(8,128)(2,1)}), bf16[64,32,512]{2,1,0:T(8,128)(2,1)S(1)}, u32[]{:S(2)}, u32[]{:S(2)}) %all-to-all-start.1) | async-done | bytes 2097184 | tf_op jit(solution)/shard_map/all_to_all | solution.py:208
  1122.4 88.7 %all-reduce.4.cloned.1.call-done = (bf16[512,3,128]{2,0,1:T(8,128)(2,1)}, bf16[128,512]{1,0:T(8,128)(2,1)}, bf16[8,512,512]{2,1,0:T(8,128)(2,1)}, bf16[8,512,512]{2,1,0:T(8,128)(2,1)}) async-done(((bf16[512,3,128]{2,0,1:T(8,128)(2,1)}, bf16[128,512]{1,0:T(8,128)(2,1)}, bf16[8,512,512]{2,1,0:T(8,128)(2,1)}, bf16[8,512,512]{2,1,0:T(8,128)(2,1)}), (bf16[512,3,128]{2,0,1:T(8,128)(2,1)}, ...) | async-done | bytes 8912912 | tf_op jit(solution)/shard_map/psum | solution.py:289
  1226.4 131.7 %reduce-scatter.11.cloned.1.call-done = bf16[256,8,512]{2,0,1:T(8,128)(2,1)} async-done(((bf16[1024,8,512]{2,0,1:T(8,128)(2,1)}), bf16[256,8,512]{2,0,1:T(8,128)(2,1)}) %reduce-scatter.11.cloned.1.call-update) | async-done | bytes 2097168 | tf_op jit(solution)/shard_map/reduce_scatter | solution.py:270
  1361.0 41.0 %all-reduce = (f32[512]{0:T(512)}, f32[512]{0:T(512)}, f32[512,8]{0,1:T(8,128)}) all-reduce(f32[512]{0:T(512)S(1)} %get-tuple-element.11, f32[512]{0:T(512)S(1)} %copy-done.53, f32[512,8]{0,1:T(8,128)S(1)} %convolution_bitcast_fusion.1), channel_id=1, replica_groups=mesh['wide'=8,'narrow'=4] {'wide','narrow'}, use_global_device_ids=true, to_apply=%region_18.19 | all-reduce | flops 5120 | bytes 40960 | tf_op jit(solution)/shard_map/psum | solution.py:294
  (210 shorter events, 281.6 us)
Async XLA Ops:
  7.2 157.5 %copy-start = (bf16[512,3,128]{2,0,1:T(8,128)(2,1)S(1)}, bf16[512,3,128]{2,0,1:T(8,128)(2,1)}, u32[]{:S(2)}) copy-start(bf16[512,3,128]{2,0,1:T(8,128)(2,1)} %param.17) | copy-start | bytes 1179652
  7.2 157.5 %all-gather.5.cloned.1.call-start = ((), (), s32[]{:S(2)}) async-start(), calls=%async_computation.8 | async-start | bytes 10485760 | tf_op jit(solution)/shard_map/all_gather | solution.py:66
  13.5 400.2 %reduce-scatter.5.cloned.1.call-start = ((), (), s32[]{:S(2)}) async-start(), calls=%async_computation.9 | async-start | bytes 10485760 | tf_op jit(solution)/shard_map/reduce_scatter | solution.py:105
  271.2 142.5 %copy-start.1 = (bf16[8,256,512]{2,1,0:T(8,128)(2,1)S(1)}, bf16[8,256,512]{2,1,0:T(8,128)(2,1)}, u32[]{:S(2)}) copy-start(bf16[8,256,512]{2,1,0:T(8,128)(2,1)} %param.12) | copy-start | bytes 6291460
  271.2 145.0 %copy-start.48 = (f32[512]{0:T(512)S(1)}, f32[512]{0:T(512)}, u32[]{:S(2)}) copy-start(f32[512]{0:T(512)} %param.19) | copy-start | bytes 6148
  416.2 273.5 %copy-start.39 = (f32[8,256]{1,0:T(8,128)}, f32[8,256]{1,0:T(8,128)S(1)}, u32[]{:S(2)}) copy-start(f32[8,256]{1,0:T(8,128)S(1)} %add_rsqrt_fusion) | copy-start | bytes 24580
  419.5 30.4 %all-to-all-start = ((bf16[8,256,512]{2,0,1:T(8,128)(2,1)}), bf16[8,256,512]{2,0,1:T(8,128)(2,1)}, u32[]{:S(2)}, u32[]{:S(2)}) async-start(bf16[8,256,512]{2,0,1:T(8,128)(2,1)} %copy.103), calls=%async_computation.1 | async-start | bytes 4194304 | tf_op jit(solution)/shard_map/all_to_all | solution.py:119
  424.8 82.5 %all-gather.7.cloned.1.call-start = ((), (), s32[]{:S(2)}) async-start(), calls=%async_computation.10 | async-start | bytes 2621440 | tf_op jit(solution)/shard_map/all_gather | solution.py:148
  424.9 225.6 %copy-start.31 = (s32[32,2,56]{2,1,0:T(2,128)}, s32[32,2,56]{2,1,0:T(2,128)S(1)}, u32[]{:S(2)}) copy-start(s32[32,2,56]{2,1,0:T(2,128)S(1)} %copy.101) | copy-start | bytes 43012
  425.2 225.4 %copy-start.35 = (pred[32,2,56]{2,1,0:T(4,128)(4,1)}, pred[32,2,56]{2,1,0:T(4,128)(4,1)S(1)}, u32[]{:S(2)}) copy-start(pred[32,2,56]{2,1,0:T(4,128)(4,1)S(1)} %copy.100) | copy-start | bytes 10756
  457.8 190.3 %copy-start.22 = (bf16[64,56,8]{1,2,0:T(8,128)(2,1)}, bf16[64,56,8]{1,2,0:T(8,128)(2,1)S(1)}, u32[]{:S(2)}) copy-start(bf16[64,56,8]{1,2,0:T(8,128)(2,1)S(1)} %fusion.112) | copy-start | bytes 172036
  461.5 92.4 %all-gather.9.cloned.1.call-start = ((), (), s32[]{:S(2)}) async-start(), calls=%async_computation.12 | async-start | bytes 2621440 | tf_op jit(solution)/shard_map/all_gather | solution.py:177
  502.6 95.9 %reduce-scatter.7.cloned.1.call-start = ((), (), s32[]{:S(2)}) async-start(), calls=%async_computation.11 | async-start | bytes 2621440 | tf_op jit(solution)/shard_map/reduce_scatter | solution.py:154
  516.7 127.8 %reduce-scatter.9.cloned.1.call-start = ((), (), s32[]{:S(2)}) async-start(), calls=%async_computation.13 | async-start | bytes 2621440 | tf_op jit(solution)/shard_map/reduce_scatter | solution.py:183
  566.2 275.4 %all-gather.11.cloned.1.call-start = ((), (), s32[]{:S(2)}) async-start(), calls=%async_computation.14 | async-start | bytes 10485760 | tf_op jit(solution)/shard_map/all_gather | solution.py:216
  693.3 517.8 %all-reduce.4.cloned.1.call-start = ((), (), s32[]{:S(2)}) async-start(), calls=%async_computation.16 | async-start | bytes 17825792 | tf_op jit(solution)/shard_map/psum | solution.py:289
  694.4 154.6 %copy-start.33 = (f32[2,8,512]{2,1,0:T(8,128)}, f32[2,8,512]{2,1,0:T(8,128)S(1)}, u32[]{:S(2)}) copy-start(f32[2,8,512]{2,1,0:T(8,128)S(1)} %log_add_fusion.1) | copy-start | bytes 98308
  1057.4 300.7 %reduce-scatter.11.cloned.1.call-start = ((), (), s32[]{:S(2)}) async-start(), calls=%async_computation.15 | async-start | bytes 10485760 | tf_op jit(solution)/shard_map/reduce_scatter | solution.py:270
  1076.7 43.1 %all-to-all-start.1 = ((bf16[64,32,512]{2,1,0:T(8,128)(2,1)}), bf16[64,32,512]{2,1,0:T(8,128)(2,1)S(1)}, u32[]{:S(2)}, u32[]{:S(2)}) async-start(bf16[64,32,512]{2,1,0:T(8,128)(2,1)} %copy.107), calls=%async_computation.3 | async-start | bytes 4194304 | tf_op jit(solution)/shard_map/all_to_all | solution.py:208
  1221.8 136.3 %copy-start.43 = (f32[8,256]{1,0:T(8,128)S(1)}, f32[8,256]{1,0:T(8,128)}, u32[]{:S(2)}) copy-start(f32[8,256]{1,0:T(8,128)} %copy-done.42) | copy-start | bytes 24580
  1221.8 136.3 %copy-start.52 = (f32[512]{0:T(512)S(1)}, f32[512]{0:T(512)}, u32[]{:S(2)}) copy-start(f32[512]{0:T(512)} %param.16) | copy-start | bytes 6148
  1226.4 175.7 %copy-start.40 = (f32[8,256]{1,0:T(8,128)S(1)}, f32[8,256]{1,0:T(8,128)}, u32[]{:S(2)}) copy-start(f32[8,256]{1,0:T(8,128)} %copy-done.39) | copy-start | bytes 24580
  1226.4 175.7 %copy-start.45 = (f32[8,256]{1,0:T(8,128)S(1)}, f32[8,256]{1,0:T(8,128)}, u32[]{:S(2)}) copy-start(f32[8,256]{1,0:T(8,128)} %copy-done.44) | copy-start | bytes 24580
  1226.4 175.7 %copy-start.49 = (f32[512]{0:T(512)S(1)}, f32[512]{0:T(512)}, u32[]{:S(2)}) copy-start(f32[512]{0:T(512)} %param.19) | copy-start | bytes 6148
  (43 other events, 530.9 us)
Sparse Core Ops, SparseCore 0:
  13.6 151.0 all-gather.4
  271.4 142.2 reduce-scatter.4
  461.6 45.5 all-gather.6
  509.2 44.6 all-gather.8
  556.1 42.4 reduce-scatter.6
  601.4 43.1 reduce-scatter.8
  693.4 148.1 all-gather.10
  1057.6 153.5 all-reduce.3
  1213.6 144.4 reduce-scatter.10
where the time goes:
time: 1430 us; the launch traced here: 1420 us
  waiting for transfers between devices  816 us (57%)
  matrix products  298 us (21%)
  other arithmetic  136 us (10%)
  blocking collectives  99.7 us (7%)
  local copies, waits for them, and re-layouts  42.3 us (3%)
  between operations  14.7 us (1%)
    all_gather x1, waiting for transfers between devices, per_device(): lax.all_gather(normed_one.astype(jnp.bfloat16), 'narrow', axis=1, tiled=T...  143 us
    reduce_scatter x1, waiting for transfers between devices, per_device(): lax.psum_scatter(jnp.einsum('pbi,iq->pbq', current_row_block, output_proj...  142 us
    all_gather x1, waiting for transfers between devices, per_device(): lax.all_gather(grad_hidden.astype(jnp.bfloat16), 'narrow', axis=1, tiled=...  136 us
    reduce_scatter x1, waiting for transfers between devices, per_device(): lax.psum_scatter(jnp.einsum('slcf,dcf->lsd', current_row_block, input_pro...  132 us
    psum x1, waiting for transfers between devices, per_device(): lax.psum(inproj_grad.astype(jnp.bfloat16), 'wide').astype(jnp.float32)  88.7 us
    convert_element_type x2, other arithmetic, per_device(): (probabilities * (grad_probs - row_inner)).astype(jnp.bfloat16)  55.9 us
    dot_general x2, matrix products, per_device(): jnp.einsum('qshd,skhd->shqk', grad_out_block, values_local, preferred_ele...  45.8 us
    psum x1, blocking collectives, per_device(): lax.psum((gain_one_grad, gain_two_grad, router_grad), ('wide', 'narrow'))  41 us
  transfers between devices with their start and end apart: 11, of which 11 were waited for; matrix products, arithmetic and copies ran while one was open for 6% of the time, Pallas kernels for 0%

commit v1 on v0

v1 whole, which is shorter than its diff:
```python
import functools

import jax
import jax.numpy as jnp
from jax import lax
from jax.experimental import pallas as pl
from jax.experimental.pallas import tpu as pltpu
from jax.sharding import PartitionSpec as P

MESH = pl.DeviceIdType.MESH
HEAD_DIM = 64
PAIR = 2 * HEAD_DIM
EPS = 1e-06
NEG = -1e30
bf16 = jnp.bfloat16
f32 = jnp.float32
VMEM_LIMIT = 56 << 20


def nn(a, b):
    return lax.dot_general(a, b, (((1,), (0,)), ((), ())), preferred_element_type=f32)


def nt(a, b):
    return lax.dot_general(a, b, (((1,), (1,)), ((), ())), preferred_element_type=f32)


def tn(a, b):
    return lax.dot_general(a, b, (((0,), (0,)), ((), ())), preferred_element_type=f32)


def whole(memory=pltpu.VMEM):
    return pl.BlockSpec(memory_space=memory)


def peers(kind, narrow, wide, cluster):
    w, z = lax.axis_index("wide"), lax.axis_index("narrow")
    if kind == "narrow":
        return z, narrow, lambda j: (w, j)
    if kind == "wide":
        return w, wide, lambda j: (j, z)
    if kind == "cluster":
        first = (w // cluster) * cluster
        return w - first, cluster, lambda j: (first + j, z)
    return w * narrow + z, wide * narrow, lambda j: (j // narrow, lax.rem(j, narrow))


def exchange_body(plans, sizes, *refs):
    count = len(plans)
    sources, targets, sems = refs[:count], refs[count : 2 * count], refs[2 * count :]
    barrier = pltpu.get_barrier_semaphore()
    groups = [peers(kind, *sizes) for kind, _, _, _ in plans]
    greeted = 0
    for kind in dict.fromkeys(kind for kind, _, _, _ in plans):
        me, total, place = peers(kind, *sizes)

        def greet(k, carry, me=me, total=total, place=place):
            pl.semaphore_signal(
                barrier, inc=1, device_id=place(lax.rem(me + k, total)), device_id_type=MESH
            )
            return carry

        lax.fori_loop(1, total, greet, 0)
        greeted += total - 1
    pl.semaphore_wait(barrier, greeted)

    def copy_of(i, k):
        (me, total, place), (_, source_at, target_at, _) = groups[i], plans[i]
        j = lax.rem(me + k, total)
        return pltpu.make_async_remote_copy(
            src_ref=source_at(sources[i], j),
            dst_ref=target_at(targets[i], me),
            send_sem=sems[3 * i].at[k],
            recv_sem=sems[3 * i + 1].at[k],
            device_id=place(j),
            device_id_type=MESH,
        )

    def own_of(i):
        me = groups[i][0]
        return pltpu.make_async_copy(
            plans[i][1](sources[i], me), plans[i][2](targets[i], me), sems[3 * i + 2]
        )

    for i in range(count):

        def begin(k, carry, i=i):
            copy_of(i, k).start()
            return carry

        lax.fori_loop(1, groups[i][1], begin, 0)
        own_of(i).start()
    for i in range(count):

        def finish(k, carry, i=i):
            copy_of(i, k).wait()
            return carry

        lax.fori_loop(1, groups[i][1], finish, 0)
        own_of(i).wait()


def exchange(plans, arrays, sizes, number):
    scratch = []
    for kind, _, _, _ in plans:
        total = {"narrow": sizes[0], "wide": sizes[1], "cluster": sizes[2]}.get(
            kind, sizes[0] * sizes[1]
        )
        scratch += [pltpu.SemaphoreType.DMA((total,))] * 2 + [pltpu.SemaphoreType.DMA]
    return pl.pallas_call(
        functools.partial(exchange_body, plans, sizes),
        out_shape=[jax.ShapeDtypeStruct(p[3], a.dtype) for p, a in zip(plans, arrays)],
        in_specs=[whole(pl.ANY)] * len(plans),
        out_specs=[whole(pl.ANY)] * len(plans),
        scratch_shapes=scratch,
        compiler_params=pltpu.CompilerParams(collective_id=number, has_side_effects=True),
    )(*arrays)


def rows_of(first, count, size):
    return pl.ds(pl.multiple_of(first * size, size), count * size)


def unit_of(values):
    scaling = lax.rsqrt(jnp.mean(values * values, axis=-1, keepdims=True) + EPS)
    return values * scaling, scaling


def unit_back(grad_rows, unit_rows, scaling, gain):
    grad_unit = grad_rows * gain
    inner = jnp.mean(grad_unit * unit_rows, axis=-1, keepdims=True)
    return scaling * (grad_unit - unit_rows * inner)


def attend_body(block, x_ref, start_ref, gain_ref, wall_ref, qkv_ref, att_ref, hid_ref, lse_ref, lse_acc):
    seqs, length, _ = x_ref.shape
    pairs = wall_ref.shape[0]
    lane = lax.broadcasted_iota(jnp.int32, (block, PAIR), 1)
    for s in range(seqs):
        values = x_ref[s].astype(f32)
        normed = (unit_of(values)[0] * gain_ref[...]).astype(bf16)

        def one_pair(n, carry):
            proj = nn(normed, wall_ref[n, :, : 3 * PAIR]).astype(bf16)
            qkv_ref[s, n] = proj
            keys, vals = proj[:, PAIR : 2 * PAIR], proj[:, 2 * PAIR :]
            for i in range(length // block):
                rows = slice(i * block, (i + 1) * block)
                end = (i + 1) * block
                query = proj[rows, :PAIR] * jnp.asarray(HEAD_DIM**-0.5, bf16)
                key_at = lax.broadcasted_iota(jnp.int32, (block, end), 1)
                row_at = i * block + lax.broadcasted_iota(jnp.int32, (block, end), 0)
                allowed = (key_at >= start_ref[s, rows, :]) & (key_at <= row_at)
                got = []
                for j in range(2):
                    own = (lane // HEAD_DIM) == j
                    score = nt(jnp.where(own, query, jnp.zeros_like(query)), keys[:end])
                    score = jnp.where(allowed, score, NEG)
                    peak = jnp.max(score, axis=1, keepdims=True)
                    expo = jnp.exp(score - peak)
                    total = jnp.sum(expo, axis=1, keepdims=True)
                    got.append(nn(expo.astype(bf16), vals[:end]) / total)
                    lse_acc[rows, :] = jnp.where(
                        lane == 2 * n + j, peak + jnp.log(total), lse_acc[rows, :]
                    )
                att_ref[s, n, rows, :] = jnp.where(lane < HEAD_DIM, got[0], got[1]).astype(bf16)
            return carry

        lax.fori_loop(0, pairs, one_pair, 0)
        hidden = values
        for n in range(pairs):
            hidden = hidden + nt(att_ref[s, n], wall_ref[n, :, 3 * PAIR :])
        hid_ref[s] = hidden.astype(bf16)
        lse_ref[s] = jnp.transpose(lse_acc[...])[: 2 * pairs]


def attend(x, start_col, gain, wall):
    seqs, length, features = x.shape
    pairs = wall.shape[0]
    return pl.pallas_call(
        functools.partial(attend_body, min(256, length)),
        out_shape=[
            jax.ShapeDtypeStruct((seqs, pairs, length, 3 * PAIR), bf16),
            jax.ShapeDtypeStruct((seqs, pairs, length, PAIR), bf16),
            jax.ShapeDtypeStruct((seqs, length, features), bf16),
            jax.ShapeDtypeStruct((seqs, 2 * pairs, length), f32),
        ],
        in_specs=[whole()] * 4,
        out_specs=[whole()] * 4,
        scratch_shapes=[pltpu.VMEM((length, PAIR), f32)],
        compiler_params=pltpu.CompilerParams(vmem_limit_bytes=VMEM_LIMIT),
    )(x, start_col, gain, wall)


def attend_back_body(
    block,
    x_ref,
    start_ref,
    gain_ref,
    wall_ref,
    qkv_ref,
    att_ref,
    lse_ref,
    dh_ref,
    gx_ref,
    gwall_ref,
    ggain_ref,
    dq_acc,
    dproj_ref,
    gn_acc,
):
    seqs, length, _ = x_ref.shape
    pairs = wall_ref.shape[0]
    lane = lax.broadcasted_iota(jnp.int32, (length, PAIR), 1)
    scale = jnp.asarray(HEAD_DIM**-0.5, bf16)
    for s in range(seqs):
        values = x_ref[s].astype(f32)
        unit, scaling = unit_of(values)
        normed = (unit * gain_ref[...]).astype(bf16)
        gn_acc[...] = jnp.zeros_like(gn_acc)

        def one_pair(n, carry):
            dh = dh_ref[s]
            d_att = nn(dh, wall_ref[n, :, 3 * PAIR :]).astype(bf16)
            att = att_ref[s, n]
            g_out = tn(dh, att)
            prod = (d_att.astype(f32) * att.astype(f32)).astype(bf16)
            head_row = lax.broadcasted_iota(jnp.int32, (8, PAIR), 0)
            head_lane = lax.broadcasted_iota(jnp.int32, (8, PAIR), 1) // HEAD_DIM
            inner = nt((head_row == head_lane).astype(bf16), prod)
            query = qkv_ref[s, n, :, :PAIR] * scale
            keys, vals = qkv_ref[s, n, :, PAIR : 2 * PAIR], qkv_ref[s, n, :, 2 * PAIR :]
            zero = jnp.zeros_like(query)
            own = [(lane // HEAD_DIM) == j for j in range(2)]
            q_own = [jnp.where(o, query, zero) for o in own]
            k_own = [jnp.where(o, keys, zero) for o in own]
            d_own = [jnp.where(o, d_att, zero) for o in own]
            lse = lse_ref[s]
            head_at = lax.broadcasted_iota(jnp.int32, lse.shape, 0)
            lse_own = [
                jnp.sum(jnp.where(head_at == 2 * n + j, lse, 0.0), axis=0, keepdims=True)
                for j in range(2)
            ]
            dq_acc[...] = jnp.zeros_like(dq_acc)
            for i in range(length // block):
                rows, first = slice(i * block, (i + 1) * block), i * block
                shape = (block, length - first)
                key_at = first + lax.broadcasted_iota(jnp.int32, shape, 0)
                row_at = first + lax.broadcasted_iota(jnp.int32, shape, 1)
                allowed = (key_at >= start_ref[s, :, first:]) & (key_at <= row_at)
                dk = dv = None
                for j in range(2):
                    score = nt(keys[rows], q_own[j][first:])
                    prob = jnp.where(allowed, jnp.exp(score - lse_own[j][:, first:]), 0.0)
                    d_prob = nt(vals[rows], d_own[j][first:])
                    d_score = (prob * (d_prob - inner[j : j + 1, first:])).astype(bf16)
                    dv_part = nn(prob.astype(bf16), d_own[j][first:])
                    dk_part = nn(d_score, q_own[j][first:])
                    dv = dv_part if dv is None else dv + dv_part
                    dk = dk_part if dk is None else dk + dk_part
                    dq_acc[first:, :] += tn(d_score, k_own[j][rows])
                dproj_ref[rows, PAIR : 2 * PAIR] = dk.astype(bf16)
                dproj_ref[rows, 2 * PAIR :] = dv.astype(bf16)
            dproj_ref[:, :PAIR] = (dq_acc[...] * HEAD_DIM**-0.5).astype(bf16)
            d_proj = dproj_ref[...]
            gn_acc[...] += nt(d_proj, wall_ref[n, :, : 3 * PAIR])
            g_in = tn(normed, d_proj)
            if s == 0:
                gwall_ref[n, :, : 3 * PAIR] = g_in
                gwall_ref[n, :, 3 * PAIR :] = g_out
            else:
                gwall_ref[n, :, : 3 * PAIR] += g_in
                gwall_ref[n, :, 3 * PAIR :] += g_out
            return carry

        lax.fori_loop(0, pairs, one_pair, 0)
        grad = gn_acc[...]
        g_gain = jnp.sum(grad * unit, axis=0, keepdims=True)
        if s == 0:
            ggain_ref[...] = g_gain
        else:
            ggain_ref[...] += g_gain
        back = unit_back(grad, unit, scaling, gain_ref[...])
        gx_ref[s] = (dh_ref[s].astype(f32) + back).astype(bf16)


def attend_back(x, start_row, gain, wall, qkv, att, lse, dh):
    seqs, length, features = x.shape
    pairs = wall.shape[0]
    return pl.pallas_call(
        functools.partial(attend_back_body, min(256, length)),
        out_shape=[
            jax.ShapeDtypeStruct((seqs, length, features), bf16),
            jax.ShapeDtypeStruct((pairs, features, 4 * PAIR), f32),
            jax.ShapeDtypeStruct((1, features), f32),
        ],
        in_specs=[whole()] * 8,
        out_specs=[whole()] * 3,
        scratch_shapes=[
            pltpu.VMEM((length, PAIR), f32),
            pltpu.VMEM((length, 3 * PAIR), bf16),
            pltpu.VMEM((length, features), f32),
        ],
        compiler_params=pltpu.CompilerParams(vmem_limit_bytes=VMEM_LIMIT),
    )(x, start_row, gain, wall, qkv, att, lse, dh)


def mix_weights(logits, key_row, experts):
    columns = logits.shape[1]
    cells = 64
    spread = jnp.broadcast_to(logits[:, None, :], (experts, cells, columns)).reshape(
        experts * cells, columns
    )
    row = lax.broadcasted_iota(jnp.int32, (experts * cells, columns), 0)
    spread = jnp.where(lax.rem(row, cells) == key_row, spread, NEG)
    expo = jnp.exp(spread - jnp.max(spread, axis=1, keepdims=True))
    return expo / jnp.sum(expo, axis=1, keepdims=True)


def mix_body(x_ref, g_ref, key_ref, gain_ref, router_ref, mixed_ref, gexp_ref, w_ref):
    experts = router_ref.shape[0]
    values = x_ref[...].astype(f32)
    normed = (unit_of(values)[0] * gain_ref[...]).astype(bf16)
    weights = mix_weights(nt(router_ref[...], normed), key_ref[...], experts)
    w_ref[...] = weights
    low = weights.astype(bf16)
    mixed_ref[...] = nn(low, normed).astype(bf16)
    gexp_ref[...] = nn(low, g_ref[...]).astype(bf16)


def mix(x, g, key_row, gain, router):
    rows = router.shape[0] * 64
    tokens, features = x.shape
    return pl.pallas_call(
        mix_body,
        out_shape=[
            jax.ShapeDtypeStruct((rows, features), bf16),
            jax.ShapeDtypeStruct((rows, features), bf16),
            jax.ShapeDtypeStruct((rows, tokens), f32),
        ],
        in_specs=[whole()] * 5,
        out_specs=[whole()] * 3,
        compiler_params=pltpu.CompilerParams(vmem_limit_bytes=VMEM_LIMIT),
    )(x, g, key_row, gain, router)


def expert_body(m_ref, g_ref, up_ref, down_ref, out_ref, gm_ref, gup_ref, gdown_ref):
    parts = up_ref.shape[0]
    rows, grads = m_ref[...], g_ref[...]
    out = gm = None
    for h in range(parts):
        pre = nn(rows, up_ref[h])
        square = pre * pre
        inner = 0.7978845608028654 * (pre + 0.044715 * pre * square)
        tanh = jnp.tanh(inner)
        act = 0.5 * pre * (1.0 + tanh)
        slope = 0.5 * (1.0 + tanh) + 0.5 * pre * (1.0 - tanh * tanh) * (
            0.7978845608028654 * (1.0 + 3 * 0.044715 * square)
        )
        low = act.astype(bf16)
        g_pre = (nt(grads, down_ref[h]) * slope).astype(bf16)
        out_part, gm_part = nn(low, down_ref[h]), nt(g_pre, up_ref[h])
        out = out_part if out is None else out + out_part
        gm = gm_part if gm is None else gm + gm_part
        gup_ref[h] = tn(rows, g_pre).astype(bf16)
        gdown_ref[h] = tn(low, grads).astype(bf16)
    out_ref[...] = out.astype(bf16)
    gm_ref[...] = gm.astype(bf16)


def expert(rows, grads, up, down):
    return pl.pallas_call(
        expert_body,
        out_shape=[jax.ShapeDtypeStruct(a.shape, bf16) for a in (rows, grads, up, down)],
        in_specs=[whole()] * 4,
        out_specs=[whole()] * 4,
        compiler_params=pltpu.CompilerParams(vmem_limit_bytes=VMEM_LIMIT),
    )(rows, grads, up, down)


def mix_back_body(
    x_ref, g_ref, gain_ref, router_ref, w_ref, eo_ref, gm_ref, out_ref, gh_ref, ggain_ref, grouter_ref
):
    experts = router_ref.shape[0]
    values = x_ref[...].astype(f32)
    unit, scaling = unit_of(values)
    normed = (unit * gain_ref[...]).astype(bf16)
    weights = w_ref[...]
    low = weights.astype(bf16)
    low_t = jnp.transpose(low)
    out_ref[...] = (values + nn(low_t, eo_ref[...])).astype(bf16)
    g_weights = nt(eo_ref[...], g_ref[...]) + nt(gm_ref[...], normed)
    inner = jnp.sum(weights * g_weights, axis=1, keepdims=True)
    g_logits = weights * (g_weights - inner)
    columns = g_logits.shape[1]
    g_logits = jnp.sum(g_logits.reshape(experts, 64, columns), axis=1).astype(bf16)
    g_normed = nn(low_t, gm_ref[...]) + tn(g_logits, router_ref[...])
    grouter_ref[...] = nn(g_logits, normed)
    ggain_ref[...] = jnp.sum(g_normed * unit, axis=0, keepdims=True)
    back = unit_back(g_normed, unit, scaling, gain_ref[...])
    gh_ref[...] = (g_ref[...].astype(f32) + back).astype(bf16)


def mix_back(x, g, gain, router, weights, eo, gm):
    return pl.pallas_call(
        mix_back_body,
        out_shape=[
            jax.ShapeDtypeStruct(x.shape, bf16),
            jax.ShapeDtypeStruct(x.shape, bf16),
            jax.ShapeDtypeStruct((1, x.shape[1]), f32),
            jax.ShapeDtypeStruct(router.shape, f32),
        ],
        in_specs=[whole()] * 7,
        out_specs=[whole()] * 4,
        compiler_params=pltpu.CompilerParams(vmem_limit_bytes=VMEM_LIMIT),
    )(x, g, gain, router, weights, eo, gm)


def per_device(
    inputs,
    positions,
    members_index,
    members_mask,
    gain_attn,
    input_projection_weight,
    output_projection_weight,
    gain_mixer,
    weight_router,
    weight_up,
    weight_down,
    cotangent,
):
    narrow, wide = lax.axis_size("narrow"), lax.axis_size("wide")
    w, z = lax.axis_index("wide"), lax.axis_index("narrow")
    seq_dev, local_len, features = inputs.shape
    length = positions.shape[1]
    groups = members_index.shape[1]
    experts = weight_up.shape[0]
    own_seqs = seq_dev // narrow
    pos_dev = local_len // wide
    seq_total = seq_dev * wide
    sizes = (narrow, wide, experts)

    wall = jnp.concatenate(
        [
            input_projection_weight.reshape(features, -1),
            jnp.transpose(output_projection_weight),
        ],
        axis=1,
    )
    wall = lax.all_gather(wall, "narrow", axis=0, tiled=False)
    e = lax.rem(w, experts)
    up_full = lax.all_gather(
        lax.dynamic_index_in_dim(weight_up, e, 0, keepdims=False), "narrow", axis=0, tiled=False
    )
    down_full = lax.all_gather(
        lax.dynamic_index_in_dim(weight_down, e, 0, keepdims=False), "narrow", axis=0, tiled=False
    )

    row_pos = lax.dynamic_slice_in_dim(positions, z * own_seqs, own_seqs, 0)
    starts = jnp.arange(length, dtype=jnp.int32)[None, :] - row_pos
    offset_rows = w * pos_dev
    index_rows = lax.dynamic_slice_in_dim(members_index, offset_rows, pos_dev, 0)
    live = lax.dynamic_slice_in_dim(members_mask, offset_rows, pos_dev, 0) > 0
    named = (
        index_rows[..., None] == jnp.arange(seq_total, dtype=jnp.int32)[None, None, None, :]
    ) & live[..., None]
    group_of = jnp.max(
        jnp.where(named, jnp.arange(groups, dtype=jnp.int32)[None, :, None, None], 0), axis=(1, 2)
    )
    key_row = group_of + groups * jnp.arange(pos_dev, dtype=jnp.int32)[:, None]
    key_row = jnp.transpose(key_row).reshape(1, seq_total * pos_dev)

    gain_one, gain_two = gain_attn.reshape(1, features), gain_mixer.reshape(1, features)
    router = jnp.transpose(weight_router)

    x_seq, g_mix = exchange(
        [
            (
                "narrow",
                lambda r, j: r.at[pl.ds(j * own_seqs, own_seqs)],
                lambda r, j: r.at[:, rows_of(j, 1, local_len)],
                (own_seqs, length, features),
            ),
            (
                "wide",
                lambda r, j: r.at[:, rows_of(j, 1, pos_dev)],
                lambda r, j: r.at[pl.ds(j * seq_dev, seq_dev)],
                (seq_total, pos_dev, features),
            ),
        ],
        [inputs, cotangent],
        sizes,
        1,
    )
    qkv, att, hidden, lse = attend(x_seq, starts[:, :, None], gain_one, wall)
    (x_mix,) = exchange(
        [
            (
                "all",
                lambda r, j: r.at[:, rows_of(lax.rem(j, narrow) * wide + j // narrow, 1, pos_dev)],
                lambda r, j: r.at[pl.ds(j * own_seqs, own_seqs)],
                (seq_total, pos_dev, features),
            )
        ],
        [hidden],
        sizes,
        2,
    )
    x_mix = x_mix.reshape(seq_total * pos_dev, features)
    g_mix = g_mix.reshape(seq_total * pos_dev, features)
    mixed, g_exp, weights = mix(x_mix, g_mix, key_row, gain_two, router)
    cells = pos_dev * groups

    def swap(a, b, number):
        shape = (experts, cells, features)
        plan = ("cluster", lambda r, j: r.at[j], lambda r, j: r.at[j], shape)
        a, b = exchange([plan, plan], [a.reshape(shape), b.reshape(shape)], sizes, number)
        return a.reshape(-1, features), b.reshape(-1, features)

    rows, row_grads = swap(mixed, g_exp, 3)
    eo, gm, g_up, g_down = expert(rows, row_grads, up_full, down_full)
    eo, gm = swap(eo, gm, 4)
    out_mix, gh_mix, g_gain_two, g_router = mix_back(
        x_mix, g_mix, gain_two, router, weights, eo, gm
    )
    dh, outputs = exchange(
        [
            (
                "all",
                lambda r, j: r.at[pl.ds(j * own_seqs, own_seqs)],
                lambda r, j: r.at[:, rows_of(lax.rem(j, narrow) * wide + j // narrow, 1, pos_dev)],
                (own_seqs, length, features),
            ),
            (
                "wide",
                lambda r, j: r.at[pl.ds(j * seq_dev, seq_dev)],
                lambda r, j: r.at[:, rows_of(j, 1, pos_dev)],
                inputs.shape,
            ),
        ],
        [
            gh_mix.reshape(seq_total, pos_dev, features),
            out_mix.reshape(seq_total, pos_dev, features),
        ],
        sizes,
        5,
    )
    gx, g_wall, g_gain_one = attend_back(
        x_seq, starts[:, None, :], gain_one, wall, qkv, att, lse, dh
    )
    (gx,) = exchange(
        [
            (
                "narrow",
                lambda r, j: r.at[:, rows_of(j, 1, local_len)],
                lambda r, j: r.at[pl.ds(j * own_seqs, own_seqs)],
                inputs.shape,
            )
        ],
        [gx],
        sizes,
        6,
    )
    grad_inputs = gx.astype(f32)

    def expert_grad(part):
        part = lax.psum_scatter(part, "narrow", scatter_dimension=0, tiled=False)
        part = lax.all_gather(part, "wide", axis=0, tiled=False)
        return jnp.sum(
            part.reshape((wide // experts, experts) + part.shape[1:]).astype(f32), axis=0
        )

    grad_up, grad_down = expert_grad(g_up), expert_grad(g_down)
    g_wall = lax.psum_scatter(g_wall.astype(bf16), "narrow", scatter_dimension=0, tiled=False)
    g_wall = lax.psum(g_wall, "wide").astype(f32)
    g_inproj = g_wall[:, : 3 * PAIR].reshape(input_projection_weight.shape)
    g_outproj = jnp.transpose(g_wall[:, 3 * PAIR :])
    g_gain_one, g_gain_two, g_router = lax.psum(
        (g_gain_one, g_gain_two, g_router), ("wide", "narrow")
    )
    return (
        outputs,
        grad_inputs,
        g_gain_one.reshape(features),
        g_inproj,
        g_outproj,
        g_gain_two.reshape(features),
        jnp.transpose(g_router),
        grad_up,
        grad_down,
    )


def solution(mesh):
    in_specs = (
        P("wide", "narrow", None),
        P("wide", None),
        P("narrow", None, None),
        P("narrow", None, None),
        P(),
        P(None, None, "narrow"),
        P("narrow", None),
        P(),
        P(),
        P(None, None, "narrow"),
        P(None, "narrow", None),
        P("wide", "narrow", None),
    )
    out_specs = (
        P("wide", "narrow", None),
        P("wide", "narrow", None),
        P(),
        P(None, None, "narrow"),
        P("narrow", None),
        P(),
        P(),
        P(None, None, "narrow"),
        P(None, "narrow", None),
    )
    return jax.shard_map(
        per_device, mesh=mesh, in_specs=in_specs, out_specs=out_specs, check_vma=False
    )
```

time: 1430 us -> 703 us (0.49)
  waiting for transfers between devices: 816 us -> 179 us
  Pallas kernels: 0 us -> 408 us
  matrix products: 298 us -> 0 us
  other arithmetic: 136 us -> 24.2 us
  blocking collectives: 99.7 us -> 51.4 us
  local copies, waits for them, and re-layouts: 42.3 us -> 16.6 us
    pallas_call x0 -> x11, Pallas kernels: none -> 408 us  [the longest x6 277 us: exchange(): pl.pallas_call(functools.partial(exchange_body, plans, sizes), out_shape=...]
    dot_general x36 -> x0, matrix products: 294 us -> none  [the longest x2 45.8 us: per_device(): jnp.einsum('qshd,skhd->shqk', grad_out_block, values_local, preferred_ele...]
    all_gather x4 -> x5, waiting for transfers between devices: 321 us -> 44.4 us  [the longest x2 32.4 us: expert_grad(): part = lax.all_gather(part, 'wide', axis=0, tiled=False)]
    reduce_scatter x4 -> x3, waiting for transfers between devices: 346 us -> 133 us  [the longest x2 90.7 us: expert_grad(): part = lax.psum_scatter(part, 'narrow', scatter_dimension=0, tiled=False)]
    psum x1, waiting for transfers between devices: 88.7 us -> 0.01 us  [per_device(): g_wall = lax.psum(g_wall, 'wide').astype(f32)]
    all_to_all x2 -> x0, waiting for transfers between devices: 60.3 us -> none  [the longest x1 35.6 us: per_device(): lax.all_to_all(token_out, 'wide', split_axis=0, concat_axis=1, tiled=True)]
    all_to_all x2 -> x0, blocking collectives: 58.6 us -> none  [the longest x1 29.4 us: per_device(): lax.all_to_all(grad_grouped, 'wide', split_axis=0, concat_axis=1, tiled=T...]
    convert_element_type x11 -> x5, other arithmetic: 78.5 us -> 21.6 us  [the longest x2 13.5 us: expert_grad(): part.reshape((wide // experts, experts) + part.shape[1:]).astype(f32)]
  transfers between devices with their start and end apart: 11 -> 9, of which waited for: 11 -> 6; matrix products, arithmetic and copies ran while one was open for 6% -> 4% of each run, Pallas kernels for 0% -> 37%
where the time goes in v1:
time: 703 us; the launch traced here: 694 us
  Pallas kernels  408 us (58%)
  waiting for transfers between devices  179 us (25%)
  blocking collectives  51.4 us (7%)
  other arithmetic  24.2 us (3%)
  local copies, waits for them, and re-layouts  16.6 us (2%)
  between operations  14.3 us (2%)
    pallas_call x6, Pallas kernels, exchange(): pl.pallas_call(functools.partial(exchange_body, plans, sizes), out_shape=...  277 us
    reduce_scatter x2, waiting for transfers between devices, expert_grad(): part = lax.psum_scatter(part, 'narrow', scatter_dimension=0, tiled=False)  90.7 us
    pallas_call x1, Pallas kernels, attend_back(): pl.pallas_call(functools.partial(attend_back_body, min(256, length)), out...  57.6 us
    psum x1, blocking collectives, per_device(): lax.psum((g_gain_one, g_gain_two, g_router), ('wide', 'narrow'))  51.4 us
    reduce_scatter x1, waiting for transfers between devices, per_device(): lax.psum_scatter(g_wall.astype(bf16), 'narrow', scatter_dimension=0, tile...  42.5 us
    pallas_call x1, Pallas kernels, attend(): pl.pallas_call(functools.partial(attend_body, min(256, length)), out_shap...  40.6 us
    all_gather x2, waiting for transfers between devices, expert_grad(): part = lax.all_gather(part, 'wide', axis=0, tiled=False)  32.4 us
  transfers between devices with their start and end apart: 9, of which 6 were waited for; matrix products, arithmetic and copies ran while one was open for 4% of the time, Pallas kernels for 37%

profile of v1, /device:TPU:3, one launch (start us, length us, event | category | flops | bytes accessed | tf_op | source)
XLA Modules:
  0.0 694.0 jit_solution(4037683293392103089)
XLA Ops:
  10.2 1.9 constant_dynamic-slice_fusion.1
  12.2 1.9 constant_dynamic-slice_fusion
  18.2 66.1 %shard_map.187 = (bf16[2,1024,512]{2,1,0:T(8,128)(2,1)}, bf16[64,32,512]{2,1,0:T(8,128)(2,1)}) custom-call(bf16[8,256,512]{2,1,0:T(8,128)(2,1)} %refs_0_.1, bf16[8,256,512]{2,1,0:T(8,128)(2,1)} %refs_1_.1), custom_call_target="tpu_custom_call" | custom-call | tf_op jit(solution)/shard_map/pallas_call | solution.py:110
  84.3 12.0 %all-gather.15.cloned.1.call-done = bf16[2048,512]{0,1:T(8,128)(2,1)} async-done(((bf16[512,512]{0,1:T(8,128)(2,1)}), bf16[2048,512]{0,1:T(8,128)(2,1)}) %all-gather.15.cloned.1.call-update) | async-done | bytes 2097168 | tf_op jit(solution)/shard_map/all_gather | solution.py:451
  96.3 3.9 copy.53
  100.2 40.6 %shard_map.188 = (bf16[2,4,1024,384]{3,2,1,0:T(8,128)(2,1)}, bf16[2,4,1024,128]{3,2,1,0:T(8,128)(2,1)}, bf16[2,1024,512]{2,1,0:T(8,128)(2,1)}, f32[2,8,1024]{2,1,0:T(8,128)}) custom-call(bf16[2,1024,512]{2,1,0:T(8,128)(2,1)} %get-tuple-element.35.x_ref, s32[2,1024,1]{2,1,0:T(8,128)} %copy.54.start_ref, f32[1,512]{1,0:T(1,128)} %bitcast.54, ...), custom_call_target="tpu_custom_call" | custom-call | tf_op jit(solution)/shard_map/pallas_call | solution.py:180
  140.8 88.7 %shard_map.189 = bf16[64,32,512]{2,1,0:T(8,128)(2,1)} custom-call(bf16[2,1024,512]{2,1,0:T(8,128)(2,1)} %get-tuple-element.36.refs_0_), custom_call_target="tpu_custom_call" | custom-call | tf_op jit(solution)/shard_map/pallas_call | solution.py:110
  229.5 8.8 %shard_map.190 = (bf16[512,512]{1,0:T(8,128)(2,1)}, bf16[512,512]{1,0:T(8,128)(2,1)}, f32[512,2048]{1,0:T(8,128)}) custom-call(bf16[2048,512]{1,0:T(8,128)(2,1)} %bitcast.31, bf16[2048,512]{1,0:T(8,128)(2,1)} %bitcast.33, s32[1,2048]{1,0:T(1,128)} %reshape.95.key_ref, f32[1,512]{1,0:T(1,128)} %bitcast.52, bf16[8,512]{1,0:T(8,128)(2,1)} %bitcast.49), custom_call_target="tpu_custom_call" | custom-call | tf_op jit(solution)/shard_map/pallas_call | solution.py:334
  238.3 16.4 %shard_map.191 = (bf16[8,64,512]{2,1,0:T(8,128)(2,1)}, bf16[8,64,512]{2,1,0:T(8,128)(2,1)}) custom-call(bf16[8,64,512]{2,1,0:T(8,128)(2,1)} %bitcast.46, bf16[8,64,512]{2,1,0:T(8,128)(2,1)} %bitcast.47), custom_call_target="tpu_custom_call" | custom-call | tf_op jit(solution)/shard_map/pallas_call | solution.py:110
  254.7 12.2 %shard_map.192 = (bf16[512,512]{1,0:T(8,128)(2,1)}, bf16[512,512]{1,0:T(8,128)(2,1)}, bf16[4,512,512]{2,1,0:T(8,128)(2,1)}, bf16[4,512,512]{2,1,0:T(8,128)(2,1)}) custom-call(bf16[512,512]{1,0:T(8,128)(2,1)} %bitcast.39, bf16[512,512]{1,0:T(8,128)(2,1)} %bitcast.40, bf16[4,512,512]{2,1,0:T(8,128)(2,1)} %all-gather.7.cloned.1.call-done.up_ref, ...), custom_call_target="tpu_custom_call" | custom-call | tf_op jit(solution)/shard_map/pallas_call | solution.py:372
  267.0 15.7 %shard_map.193 = (bf16[8,64,512]{2,1,0:T(8,128)(2,1)}, bf16[8,64,512]{2,1,0:T(8,128)(2,1)}) custom-call(bf16[8,64,512]{2,1,0:T(8,128)(2,1)} %bitcast.44, bf16[8,64,512]{2,1,0:T(8,128)(2,1)} %bitcast.45), custom_call_target="tpu_custom_call" | custom-call | tf_op jit(solution)/shard_map/pallas_call | solution.py:110
  282.7 12.5 %shard_map.194 = (bf16[2048,512]{1,0:T(8,128)(2,1)}, bf16[2048,512]{1,0:T(8,128)(2,1)}, f32[1,512]{1,0:T(1,128)}, f32[8,512]{1,0:T(8,128)}) custom-call(bf16[2048,512]{1,0:T(8,128)(2,1)} %bitcast.32, bf16[2048,512]{1,0:T(8,128)(2,1)} %bitcast.34, f32[1,512]{1,0:T(1,128)} %bitcast.53, bf16[8,512]{1,0:T(8,128)(2,1)} %bitcast.50, ...), custom_call_target="tpu_custom_call" | custom-call | tf_op jit(solution)/shard_map/pallas_call | solution.py:405
  295.2 52.9 %shard_map.195 = (bf16[2,1024,512]{2,1,0:T(8,128)(2,1)}, bf16[8,256,512]{2,1,0:T(8,128)(2,1)}) custom-call(bf16[64,32,512]{2,1,0:T(8,128)(2,1)} %bitcast.37, bf16[64,32,512]{2,1,0:T(8,128)(2,1)} %bitcast.36), custom_call_target="tpu_custom_call" | custom-call | tf_op jit(solution)/shard_map/pallas_call | solution.py:110
  348.1 57.6 %shard_map.196 = (bf16[2,1024,512]{2,1,0:T(8,128)(2,1)}, f32[4,512,512]{2,1,0:T(8,128)}, f32[1,512]{1,0:T(1,128)}) custom-call(bf16[2,1024,512]{2,1,0:T(8,128)(2,1)} %get-tuple-element.35.x_ref, s32[2,1,1024]{2,1,0:T(1,128)} %broadcast_in_dim.27.start_ref, f32[1,512]{1,0:T(1,128)} %bitcast.55, bf16[4,512,512]{2,1,0:T(8,128)(2,1)} %bitcast.30, ...), custom_call_target="tpu_custom_call" | custom-call | tf_op jit(solution)/shard_map/pallas_call | solution.py:290
  405.7 3.8 convert_element_type.18
  410.7 42.5 %reduce-scatter.4.cloned.1.call-done = bf16[1,512,512]{2,1,0:T(8,128)(2,1)} async-done(((bf16[4,512,512]{2,1,0:T(8,128)(2,1)}), bf16[1,512,512]{2,1,0:T(8,128)(2,1)}) %reduce-scatter.4.cloned.1.call-update) | async-done | bytes 524304 | tf_op jit(solution)/shard_map/reduce_scatter | solution.py:575
  453.3 45.4 %reduce-scatter.6.cloned.1.call-done = bf16[1,512,512]{2,1,0:T(8,128)(2,1)} async-done(((bf16[4,512,512]{2,1,0:T(8,128)(2,1)}), bf16[1,512,512]{2,1,0:T(8,128)(2,1)}) %reduce-scatter.6.cloned.1.call-update) | async-done | bytes 524304 | tf_op jit(solution)/shard_map/reduce_scatter | solution.py:568
  498.7 45.3 %reduce-scatter.8.cloned.1.call-done = bf16[1,512,512]{2,1,0:T(8,128)(2,1)} async-done(((bf16[4,512,512]{2,1,0:T(8,128)(2,1)}), bf16[1,512,512]{2,1,0:T(8,128)(2,1)}) %reduce-scatter.8.cloned.1.call-update) | async-done | bytes 524304 | tf_op jit(solution)/shard_map/reduce_scatter | solution.py:568
  544.1 36.8 %shard_map.197 = bf16[8,256,512]{2,1,0:T(8,128)(2,1)} custom-call(bf16[2,1024,512]{2,1,0:T(8,128)(2,1)} %get-tuple-element.54.refs_0_), custom_call_target="tpu_custom_call" | custom-call | tf_op jit(solution)/shard_map/pallas_call | solution.py:110
  580.9 4.2 convert_element_type.17
  585.1 51.4 %all-reduce = (f32[512]{0:T(512)}, f32[512]{0:T(512)}, f32[512,8]{0,1:T(8,128)}) all-reduce(f32[512]{0:T(512)S(1)} %bitcast.57, f32[512]{0:T(512)S(1)} %bitcast.56, f32[512,8]{0,1:T(8,128)S(1)} %bitcast.51), channel_id=1, replica_groups=mesh['wide'=8,'narrow'=4] {'wide','narrow'}, use_global_device_ids=true, to_apply=%region_1.2 | all-reduce | flops 5120 | bytes 40960 | tf_op jit(solution)/shard_map/psum | solution.py:579
  640.5 6.7 convert_element_type.20
  647.3 31.9 %all-gather.13.cloned.1.call-done = bf16[8,512,512]{2,1,0:T(8,128)(2,1)} async-done(((bf16[1,512,512]{2,1,0:T(8,128)(2,1)}), bf16[8,512,512]{2,1,0:T(8,128)(2,1)}) %all-gather.13.cloned.1.call-update) | async-done | bytes 4194320 | tf_op jit(solution)/shard_map/all_gather | solution.py:569
  679.1 6.7 convert_element_type.21
  (61 shorter events, 13.8 us)
Async XLA Ops:
  7.2 89.1 %all-gather.15.cloned.1.call-start = ((), (), s32[]{:S(2)}) async-start(), calls=%async_computation.11 | async-start | bytes 2621440 | tf_op jit(solution)/shard_map/all_gather | solution.py:451
  10.1 4.1 copy-start.5
  10.2 244.6 %all-gather.7.cloned.1.call-start = ((), (), s32[]{:S(2)}) async-start(), calls=%async_computation.3 | async-start | bytes 2621440 | tf_op jit(solution)/shard_map/all_gather | solution.py:453
  10.2 5.4 copy-start.2
  10.2 5.4 copy-start.3
  12.2 242.5 %all-gather.9.cloned.1.call-start = ((), (), s32[]{:S(2)}) async-start(), calls=%async_computation.4 | async-start | bytes 2621440 | tf_op jit(solution)/shard_map/all_gather | solution.py:456
  14.1 439.1 %reduce-scatter.4.cloned.1.call-start = ((), (), s32[]{:S(2)}) async-start(), calls=%async_computation.5 | async-start | bytes 2621440 | tf_op jit(solution)/shard_map/reduce_scatter | solution.py:575
  409.5 89.2 %reduce-scatter.6.cloned.1.call-start = ((), (), s32[]{:S(2)}) async-start(), calls=%async_computation.7 | async-start | bytes 2621440 | tf_op jit(solution)/shard_map/reduce_scatter | solution.py:568
  410.1 133.9 %reduce-scatter.8.cloned.1.call-start = ((), (), s32[]{:S(2)}) async-start(), calls=%async_computation.9 | async-start | bytes 2621440 | tf_op jit(solution)/shard_map/reduce_scatter | solution.py:568
  410.7 225.8 %all-reduce.3.cloned.1.call-start = ((), (), s32[]{:S(2)}) async-start(), calls=%async_computation.6 | async-start | bytes 1048576 | tf_op jit(solution)/shard_map/psum | solution.py:576
  453.2 187.3 %all-gather.11.cloned.1.call-start = ((), (), s32[]{:S(2)}) async-start(), calls=%async_computation.8 | async-start | bytes 4718592 | tf_op jit(solution)/shard_map/all_gather | solution.py:569
  498.7 180.5 %all-gather.13.cloned.1.call-start = ((), (), s32[]{:S(2)}) async-start(), calls=%async_computation.10 | async-start | bytes 4718592 | tf_op jit(solution)/shard_map/all_gather | solution.py:569
  580.8 4.2 copy-start.4
  580.8 4.2 copy-start.6
  580.8 4.2 copy-start.7
  636.5 2.5 copy-start
  647.2 38.6 %copy-start.1 = (bf16[8,256,512]{2,1,0:T(8,128)(2,1)S(1)}, bf16[8,256,512]{2,1,0:T(8,128)(2,1)}, u32[]{:S(2)}) copy-start(bf16[8,256,512]{2,1,0:T(8,128)(2,1)} %get-tuple-element.120) | copy-start | bytes 6291460
Sparse Core Ops, SparseCore 0:
  10.3 85.9 all-gather.14
  97.9 44.6 all-gather.6
  144.2 81.8 all-gather.8
  409.6 43.5 reduce-scatter.3
  455.5 43.1 reduce-scatter.5
  500.8 43.1 reduce-scatter.7
  547.4 52.1 all-reduce.2
  601.6 38.8 all-gather.10
  642.4 36.7 all-gather.12

commit v2 on v1

--- a/solution.py
+++ b/solution.py
@@ -132,64 +132,312 @@
     return scaling * (grad_unit - unit_rows * inner)
 
 
-def attend_body(block, x_ref, start_ref, gain_ref, wall_ref, qkv_ref, att_ref, hid_ref, lse_ref, lse_acc):
-    seqs, length, _ = x_ref.shape
+def copies(kind, sizes, source_at, target_at, send, recv, own, base=0):
+    me, total, place = peers(kind, *sizes)
+
+    def copy_of(k):
+        j = lax.rem(me + k, total)
+        return pltpu.make_async_remote_copy(
+            src_ref=source_at(j),
+            dst_ref=target_at(me),
+            send_sem=send.at[base + k],
+            recv_sem=recv.at[base + k],
+            device_id=place(j),
+            device_id_type=MESH,
+        )
+
+    def each(action):
+        def step(k, carry):
+            action(copy_of(k))
+            return carry
+
+        lax.fori_loop(1, total, step, 0)
+
+    def local():
+        return pltpu.make_async_copy(source_at(me), target_at(me), own)
+
+    def start():
+        each(lambda c: c.start())
+        if own is not None:
+            local().start()
+
+    def wait_recv():
+        each(lambda c: c.wait_recv())
+        if own is not None:
+            local().wait()
+
+    def wait_send():
+        each(lambda c: c.wait_send())
+
+    return start, wait_recv, wait_send
+
+
+def greet(kinds, sizes):
+    barrier = pltpu.get_barrier_semaphore()
+    greeted = 0
+    for kind in kinds:
+        me, total, place = peers(kind, *sizes)
+
+        def step(k, carry, me=me, total=total, place=place):
+            pl.semaphore_signal(
+                barrier, inc=1, device_id=place(lax.rem(me + k, total)), device_id_type=MESH
+            )
+            return carry
+
+        lax.fori_loop(1, total, step, 0)
+        greeted += total - 1
+    pl.semaphore_wait(barrier, greeted)
+
+
+def attend_seq(block, s, x_ref, start_ref, gain_ref, wall_ref, qkv_ref, att_ref, hid_ref, lse_ref, lse_acc, stored):
+    _, length, _ = x_ref.shape
     pairs = wall_ref.shape[0]
     lane = lax.broadcasted_iota(jnp.int32, (block, PAIR), 1)
+    values = x_ref[s].astype(f32)
+    normed = (unit_of(values)[0] * gain_ref[...]).astype(bf16)
+
+    def one_pair(n, carry):
+        proj = nn(normed, wall_ref[n, :, : 3 * PAIR]).astype(bf16)
+        qkv_ref[s, n] = proj
+        keys, vals = proj[:, PAIR : 2 * PAIR], proj[:, 2 * PAIR :]
+        for i in range(length // block):
+            rows = slice(i * block, (i + 1) * block)
+            end = (i + 1) * block
+            query = proj[rows, :PAIR] * jnp.asarray(HEAD_DIM**-0.5, bf16)
+            key_at = lax.broadcasted_iota(jnp.int32, (block, end), 1)
+            row_at = i * block + lax.broadcasted_iota(jnp.int32, (block, end), 0)
+            allowed = (key_at >= start_ref[s, rows, :]) & (key_at <= row_at)
+            got = []
+            for j in range(2):
+                own = (lane // HEAD_DIM) == j
+                score = nt(jnp.where(own, query, jnp.zeros_like(query)), keys[:end])
+                score = jnp.where(allowed, score, NEG)
+                peak = jnp.max(score, axis=1, keepdims=True)
+                expo = jnp.exp(score - peak)
+                total = jnp.sum(expo, axis=1, keepdims=True)
+                got.append(nn(expo.astype(bf16), vals[:end]) / total)
+                lse_acc[rows, :] = jnp.where(
+                    lane == 2 * n + j, peak + jnp.log(total), lse_acc[rows, :]
+                )
+            att_ref[s, n, rows, :] = jnp.where(lane < HEAD_DIM, got[0], got[1]).astype(bf16)
+        stored(s, n)
+        return carry
+
+    lax.fori_loop(0, pairs, one_pair, 0)
+    hidden = values
+    for n in range(pairs):
+        hidden = hidden + nt(att_ref[s, n], wall_ref[n, :, 3 * PAIR :])
+    hid_ref[s] = hidden.astype(bf16)
+    lse_ref[s] = jnp.transpose(lse_acc[...])[: 2 * pairs]
+
+
+def forward_body(
+    sizes,
+    block,
+    inputs_ref,
+    cot_ref,
+    wall_own_ref,
+    start_ref,
+    gain_ref,
+    xmix_ref,
+    gmix_ref,
+    x_out,
+    wall_out,
+    qkv_out,
+    att_out,
+    lse_ref,
+    x_ref,
+    wall_ref,
+    qkv_ref,
+    att_ref,
+    hid_ref,
+    lse_acc,
+    x_send,
+    x_recv,
+    x_own,
+    wall_send,
+    wall_recv,
+    wall_local,
+    share_send,
+    share_recv,
+    cot_send,
+    cot_recv,
+    cot_own,
+    hid_send,
+    hid_recv,
+    hid_own,
+    out_sem,
+    keep_sem,
+):
+    narrow, wide, _ = sizes
+    w, z = lax.axis_index("wide"), lax.axis_index("narrow")
+    seqs, length, features = x_ref.shape
+    seq_dev, local_len, _ = inputs_ref.shape
+    pos_dev = local_len // wide
+    pairs = wall_ref.shape[0]
+    slice_rows = features // wide
+    mine = rows_of(w, 1, slice_rows)
+    everyone = wide * narrow
+
+    greet(["all"], sizes)
+    wall_z = copies(
+        "narrow",
+        sizes,
+        lambda j: wall_own_ref.at[mine],
+        lambda j: wall_ref.at[j, mine],
+        wall_send,
+        wall_recv,
+        wall_local,
+    )
+    wall_w = copies(
+        "wide",
+        sizes,
+        lambda j: wall_ref.at[:, mine],
+        lambda j: wall_ref.at[:, rows_of(j, 1, slice_rows)],
+        share_send,
+        share_recv,
+        None,
+    )
+    x_z = [
+        copies(
+            "narrow",
+            sizes,
+            lambda j, s=s: inputs_ref.at[j * seqs + s],
+            lambda j, s=s: x_ref.at[s, rows_of(j, 1, local_len)],
+            x_send,
+            x_recv,
+            x_own.at[s],
+            s * narrow,
+        )
+        for s in range(seqs)
+    ]
+    cot_w = copies(
+        "wide",
+        sizes,
+        lambda j: cot_ref.at[:, rows_of(j, 1, pos_dev)],
+        lambda j: gmix_ref.at[pl.ds(j * seq_dev, seq_dev)],
+        cot_send,
+        cot_recv,
+        cot_own,
+    )
+    hid_all = [
+        copies(
+            "all",
+            sizes,
+            lambda j, s=s: hid_ref.at[
+                s, rows_of(lax.rem(j, narrow) * wide + j // narrow, 1, pos_dev)
+            ],
+            lambda j, s=s: xmix_ref.at[j * seqs + s],
+            hid_send,
+            hid_recv,
+            hid_own.at[s],
+            s * everyone,
+        )
+        for s in range(seqs)
+    ]
+    wall_z[0]()
+    x_z[0][0]()
+    wall_z[1]()
+    wall_w[0]()
+    x_z[0][1]()
+    for s in range(1, seqs):
+        x_z[s][0]()
+    wall_w[1]()
+    cot_w[0]()
+
+    def kept(s, n):
+        return (
+            pltpu.make_async_copy(qkv_ref.at[s, n], qkv_out.at[s, n], out_sem.at[0, s, n]),
+            pltpu.make_async_copy(att_ref.at[s, n], att_out.at[s, n], out_sem.at[1, s, n]),
+        )
+
+    def stored(s, n):
+        for c in kept(s, n):
+            c.start()
+
+    wall_keep = pltpu.make_async_copy(wall_ref, wall_out, keep_sem.at[seqs])
+    wall_keep.start()
+    x_keep = [
+        pltpu.make_async_copy(x_ref.at[s], x_out.at[s], keep_sem.at[s]) for s in range(seqs)
+    ]
     for s in range(seqs):
-        values = x_ref[s].astype(f32)
-        normed = (unit_of(values)[0] * gain_ref[...]).astype(bf16)
-
-        def one_pair(n, carry):
-            proj = nn(normed, wall_ref[n, :, : 3 * PAIR]).astype(bf16)
-            qkv_ref[s, n] = proj
-            keys, vals = proj[:, PAIR : 2 * PAIR], proj[:, 2 * PAIR :]
-            for i in range(length // block):
-                rows = slice(i * block, (i + 1) * block)
-                end = (i + 1) * block
-                query = proj[rows, :PAIR] * jnp.asarray(HEAD_DIM**-0.5, bf16)
-                key_at = lax.broadcasted_iota(jnp.int32, (block, end), 1)
-                row_at = i * block + lax.broadcasted_iota(jnp.int32, (block, end), 0)
-                allowed = (key_at >= start_ref[s, rows, :]) & (key_at <= row_at)
-                got = []
-                for j in range(2):
-                    own = (lane // HEAD_DIM) == j
-                    score = nt(jnp.where(own, query, jnp.zeros_like(query)), keys[:end])
-                    score = jnp.where(allowed, score, NEG)
-                    peak = jnp.max(score, axis=1, keepdims=True)
-                    expo = jnp.exp(score - peak)
-                    total = jnp.sum(expo, axis=1, keepdims=True)
-                    got.append(nn(expo.astype(bf16), vals[:end]) / total)
-                    lse_acc[rows, :] = jnp.where(
-                        lane == 2 * n + j, peak + jnp.log(total), lse_acc[rows, :]
-                    )
-                att_ref[s, n, rows, :] = jnp.where(lane < HEAD_DIM, got[0], got[1]).astype(bf16)
+        if s > 0:
+            x_z[s][1]()
+        x_keep[s].start()
+        attend_seq(
+            block, s, x_ref, start_ref, gain_ref, wall_ref, qkv_ref, att_ref, hid_ref, lse_ref, lse_acc, stored
+        )
+        hid_all[s][0]()
+    wall_z[2]()
+    wall_w[2]()
+    cot_w[1]()
+    cot_w[2]()
+    wall_keep.wait()
+    for s in range(seqs):
+        x_z[s][2]()
+        x_keep[s].wait()
+
+        def settle(n, carry, s=s):
+            for c in kept(s, n):
+                c.wait()
             return carry
 
-        lax.fori_loop(0, pairs, one_pair, 0)
-        hidden = values
-        for n in range(pairs):
-            hidden = hidden + nt(att_ref[s, n], wall_ref[n, :, 3 * PAIR :])
-        hid_ref[s] = hidden.astype(bf16)
-        lse_ref[s] = jnp.transpose(lse_acc[...])[: 2 * pairs]
-
-
-def attend(x, start_col, gain, wall):
-    seqs, length, features = x.shape
-    pairs = wall.shape[0]
+        lax.fori_loop(0, pairs, settle, 0)
+    for s in range(seqs):
+        hid_all[s][1]()
+        hid_all[s][2]()
+
+
+def forward(inputs, cot, wall_own, start_col, gain, sizes, number):
+    narrow, wide, _ = sizes
+    seq_dev, local_len, features = inputs.shape
+    seqs, length, pairs = seq_dev // narrow, local_len * narrow, narrow
+    everyone = wide * narrow
+    pos_dev = local_len // wide
+    dma = pltpu.SemaphoreType.DMA
+    qkv_shape = (seqs, pairs, length, 3 * PAIR)
+    att_shape = (seqs, pairs, length, PAIR)
     return pl.pallas_call(
-        functools.partial(attend_body, min(256, length)),
+        functools.partial(forward_body, sizes, min(256, length)),
         out_shape=[
-            jax.ShapeDtypeStruct((seqs, pairs, length, 3 * PAIR), bf16),
-            jax.ShapeDtypeStruct((seqs, pairs, length, PAIR), bf16),
+            jax.ShapeDtypeStruct((seq_dev * wide, pos_dev, features), bf16),
+            jax.ShapeDtypeStruct((seq_dev * wide, pos_dev, features), bf16),
             jax.ShapeDtypeStruct((seqs, length, features), bf16),
+            jax.ShapeDtypeStruct((pairs,) + wall_own.shape, bf16),
+            jax.ShapeDtypeStruct(qkv_shape, bf16),
+            jax.ShapeDtypeStruct(att_shape, bf16),
             jax.ShapeDtypeStruct((seqs, 2 * pairs, length), f32),
         ],
-        in_specs=[whole()] * 4,
-        out_specs=[whole()] * 4,
-        scratch_shapes=[pltpu.VMEM((length, PAIR), f32)],
-        compiler_params=pltpu.CompilerParams(vmem_limit_bytes=VMEM_LIMIT),
-    )(x, start_col, gain, wall)
+        in_specs=[whole(pl.ANY)] * 3 + [whole()] * 2,
+        out_specs=[whole(pl.ANY)] * 6 + [whole()],
+        scratch_shapes=[
+            pltpu.VMEM((seqs, length, features), bf16),
+            pltpu.VMEM((pairs,) + wall_own.shape, bf16),
+            pltpu.VMEM(qkv_shape, bf16),
+            pltpu.VMEM(att_shape, bf16),
+            pltpu.VMEM((seqs, length, features), bf16),
+            pltpu.VMEM((length, PAIR), f32),
+            dma((seqs * narrow,)),
+            dma((seqs * narrow,)),
+            dma((seqs,)),
+            dma((narrow,)),
+            dma((narrow,)),
+            dma,
+            dma((wide,)),
+            dma((wide,)),
+            dma((wide,)),
+            dma((wide,)),
+            dma,
+            dma((seqs * everyone,)),
+            dma((seqs * everyone,)),
+            dma((seqs,)),
+            dma((2, seqs, pairs)),
+            dma((seqs + 1,)),
+        ],
+        compiler_params=pltpu.CompilerParams(
+            collective_id=number, has_side_effects=True, vmem_limit_bytes=VMEM_LIMIT
+        ),
+    )(inputs, cot, wall_own, start_col, gain)
 
 
 def attend_back_body(
@@ -448,7 +696,6 @@
         ],
         axis=1,
     )
-    wall = lax.all_gather(wall, "narrow", axis=0, tiled=False)
     e = lax.rem(w, experts)
     up_full = lax.all_gather(
         lax.dynamic_index_in_dim(weight_up, e, 0, keepdims=False), "narrow", axis=0, tiled=False
@@ -474,38 +721,8 @@
     gain_one, gain_two = gain_attn.reshape(1, features), gain_mixer.reshape(1, features)
     router = jnp.transpose(weight_router)
 
-    x_seq, g_mix = exchange(
-        [
-            (
-                "narrow",
-                lambda r, j: r.at[pl.ds(j * own_seqs, own_seqs)],
-                lambda r, j: r.at[:, rows_of(j, 1, local_len)],
-                (own_seqs, length, features),
-            ),
-            (
-                "wide",
-                lambda r, j: r.at[:, rows_of(j, 1, pos_dev)],
-                lambda r, j: r.at[pl.ds(j * seq_dev, seq_dev)],
-                (seq_total, pos_dev, features),
-            ),
-        ],
-        [inputs, cotangent],
-        sizes,
-        1,
-    )
-    qkv, att, hidden, lse = attend(x_seq, starts[:, :, None], gain_one, wall)
-    (x_mix,) = exchange(
-        [
-            (
-                "all",
-                lambda r, j: r.at[:, rows_of(lax.rem(j, narrow) * wide + j // narrow, 1, pos_dev)],
-                lambda r, j: r.at[pl.ds(j * own_seqs, own_seqs)],
-                (seq_total, pos_dev, features),
-            )
-        ],
-        [hidden],
-        sizes,
-        2,
+    x_mix, g_mix, x_seq, wall, qkv, att, lse = forward(
+        inputs, cotangent, wall, starts[:, :, None], gain_one, sizes, 1
     )
     x_mix = x_mix.reshape(seq_total * pos_dev, features)
     g_mix = g_mix.reshape(seq_total * pos_dev, features)

time: 703 us -> 662 us (0.942)
  Pallas kernels: 408 us -> 382 us
  waiting for transfers between devices: 179 us -> 168 us
    pallas_call x6 -> x4, Pallas kernels: 277 us -> 119 us  [exchange(): pl.pallas_call(functools.partial(exchange_body, plans, sizes), out_shape=...]
    pallas_call x1, Pallas kernels: 40.6 us -> 172 us  [forward(): pl.pallas_call(functools.partial(forward_body, sizes, min(256, length)),...]
    all_gather x1 -> x0, waiting for transfers between devices: 12 us -> none  [per_device(): wall = lax.all_gather(wall, 'narrow', axis=0, tiled=False)]
  transfers between devices with their start and end apart: 9 -> 8, of which waited for: 6 -> 5; matrix products, arithmetic and copies ran while one was open for 4% -> 3% of each run, Pallas kernels for 37% -> 36%
where the time goes in v2:
time: 662 us; the launch traced here: 653 us
  Pallas kernels  382 us (58%)
  waiting for transfers between devices  168 us (25%)
  blocking collectives  51.4 us (8%)
  other arithmetic  23.4 us (4%)
  between operations  14.9 us (2%)
  local copies, waits for them, and re-layouts  12.1 us (2%)
    pallas_call x1, Pallas kernels, forward(): pl.pallas_call(functools.partial(forward_body, sizes, min(256, length)),...  172 us
    pallas_call x4, Pallas kernels, exchange(): pl.pallas_call(functools.partial(exchange_body, plans, sizes), out_shape=...  119 us
    reduce_scatter x2, waiting for transfers between devices, expert_grad(): part = lax.psum_scatter(part, 'narrow', scatter_dimension=0, tiled=False)  91.8 us
    pallas_call x1, Pallas kernels, attend_back(): pl.pallas_call(functools.partial(attend_back_body, min(256, length)), out...  57.7 us
    psum x1, blocking collectives, per_device(): lax.psum((g_gain_one, g_gain_two, g_router), ('wide', 'narrow'))  51.4 us
    reduce_scatter x1, waiting for transfers between devices, per_device(): lax.psum_scatter(g_wall.astype(bf16), 'narrow', scatter_dimension=0, tile...  43 us
    all_gather x2, waiting for transfers between devices, expert_grad(): part = lax.all_gather(part, 'wide', axis=0, tiled=False)  32.2 us
    convert_element_type x2, other arithmetic, expert_grad(): part.reshape((wide // experts, experts) + part.shape[1:]).astype(f32)  13.5 us
  transfers between devices with their start and end apart: 8, of which 5 were waited for; matrix products, arithmetic and copies ran while one was open for 3% of the time, Pallas kernels for 36%

profile of v2, /device:TPU:3, one launch (start us, length us, event | category | flops | bytes accessed | tf_op | source)
XLA Modules:
  0.0 652.6 jit_solution(14330108817054280861)
XLA Ops:
  7.3 1.9 constant_dynamic-slice_fusion.1
  9.3 1.9 constant_dynamic-slice_fusion
  11.9 1.3 copy.59.start_ref
  16.7 171.8 %shard_map.187 = (bf16[64,32,512]{2,1,0:T(8,128)(2,1)}, bf16[64,32,512]{2,1,0:T(8,128)(2,1)}, bf16[2,1024,512]{2,1,0:T(8,128)(2,1)}, bf16[4,512,512]{2,1,0:T(8,1...) custom-call(bf16[8,256,512]{2,1,0:T(8,128)(2,1)} %inputs_ref.1, ...), custom_call_target="tpu_custom_call" | custom-call | tf_op jit(solution)/shard_map/pallas_call | solution.py:400
  188.5 8.8 %shard_map.188 = (bf16[512,512]{1,0:T(8,128)(2,1)}, bf16[512,512]{1,0:T(8,128)(2,1)}, f32[512,2048]{1,0:T(8,128)}) custom-call(bf16[2048,512]{1,0:T(8,128)(2,1)} %bitcast.28, bf16[2048,512]{1,0:T(8,128)(2,1)} %bitcast.30, s32[1,2048]{1,0:T(1,128)} %reshape.95.key_ref, f32[1,512]{1,0:T(1,128)} %bitcast.49, bf16[8,512]{1,0:T(8,128)(2,1)} %bitcast.46), custom_call_target="tpu_custom_call" | custom-call | tf_op jit(solution)/shard_map/pallas_call | solution.py:582
  197.3 15.6 %shard_map.189 = (bf16[8,64,512]{2,1,0:T(8,128)(2,1)}, bf16[8,64,512]{2,1,0:T(8,128)(2,1)}) custom-call(bf16[8,64,512]{2,1,0:T(8,128)(2,1)} %bitcast.43, bf16[8,64,512]{2,1,0:T(8,128)(2,1)} %bitcast.44), custom_call_target="tpu_custom_call" | custom-call | tf_op jit(solution)/shard_map/pallas_call | solution.py:110
  213.0 12.2 %shard_map.190 = (bf16[512,512]{1,0:T(8,128)(2,1)}, bf16[512,512]{1,0:T(8,128)(2,1)}, bf16[4,512,512]{2,1,0:T(8,128)(2,1)}, bf16[4,512,512]{2,1,0:T(8,128)(2,1)}) custom-call(bf16[512,512]{1,0:T(8,128)(2,1)} %bitcast.36, bf16[512,512]{1,0:T(8,128)(2,1)} %bitcast.37, bf16[4,512,512]{2,1,0:T(8,128)(2,1)} %all-gather.5.cloned.1.call-done.up_ref, ...), custom_call_target="tpu_custom_call" | custom-call | tf_op jit(solution)/shard_map/pallas_call | solution.py:620
  225.2 15.4 %shard_map.191 = (bf16[8,64,512]{2,1,0:T(8,128)(2,1)}, bf16[8,64,512]{2,1,0:T(8,128)(2,1)}) custom-call(bf16[8,64,512]{2,1,0:T(8,128)(2,1)} %bitcast.41, bf16[8,64,512]{2,1,0:T(8,128)(2,1)} %bitcast.42), custom_call_target="tpu_custom_call" | custom-call | tf_op jit(solution)/shard_map/pallas_call | solution.py:110
  240.6 12.6 %shard_map.192 = (bf16[2048,512]{1,0:T(8,128)(2,1)}, bf16[2048,512]{1,0:T(8,128)(2,1)}, f32[1,512]{1,0:T(1,128)}, f32[8,512]{1,0:T(8,128)}) custom-call(bf16[2048,512]{1,0:T(8,128)(2,1)} %bitcast.29, bf16[2048,512]{1,0:T(8,128)(2,1)} %bitcast.31, f32[1,512]{1,0:T(1,128)} %bitcast.50, bf16[8,512]{1,0:T(8,128)(2,1)} %bitcast.47, ...), custom_call_target="tpu_custom_call" | custom-call | tf_op jit(solution)/shard_map/pallas_call | solution.py:653
  253.2 51.4 %shard_map.193 = (bf16[2,1024,512]{2,1,0:T(8,128)(2,1)}, bf16[8,256,512]{2,1,0:T(8,128)(2,1)}) custom-call(bf16[64,32,512]{2,1,0:T(8,128)(2,1)} %bitcast.34, bf16[64,32,512]{2,1,0:T(8,128)(2,1)} %bitcast.33), custom_call_target="tpu_custom_call" | custom-call | tf_op jit(solution)/shard_map/pallas_call | solution.py:110
  304.6 57.7 %shard_map.194 = (bf16[2,1024,512]{2,1,0:T(8,128)(2,1)}, f32[4,512,512]{2,1,0:T(8,128)}, f32[1,512]{1,0:T(1,128)}) custom-call(bf16[2,1024,512]{2,1,0:T(8,128)(2,1)} %get-tuple-element.50.x_ref, s32[2,1,1024]{2,1,0:T(1,128)} %broadcast_in_dim.27.start_ref, f32[1,512]{1,0:T(1,128)} %bitcast.52, bf16[4,512,512]{2,1,0:T(8,128)(2,1)} %get-tuple-element.51.wall_ref, ...), custom_call_target="tpu_custom_call" | custom-call | tf_op jit(solution)/shard_map/pallas_call | solution.py:538
  362.3 3.8 convert_element_type.18
  367.3 43.0 %reduce-scatter.4.cloned.1.call-done = bf16[1,512,512]{2,1,0:T(8,128)(2,1)} async-done(((bf16[4,512,512]{2,1,0:T(8,128)(2,1)}), bf16[1,512,512]{2,1,0:T(8,128)(2,1)}) %reduce-scatter.4.cloned.1.call-update) | async-done | bytes 524304 | tf_op jit(solution)/shard_map/reduce_scatter | solution.py:792
  410.4 46.0 %reduce-scatter.6.cloned.1.call-done = bf16[1,512,512]{2,1,0:T(8,128)(2,1)} async-done(((bf16[4,512,512]{2,1,0:T(8,128)(2,1)}), bf16[1,512,512]{2,1,0:T(8,128)(2,1)}) %reduce-scatter.6.cloned.1.call-update) | async-done | bytes 524304 | tf_op jit(solution)/shard_map/reduce_scatter | solution.py:785
  456.4 45.8 %reduce-scatter.8.cloned.1.call-done = bf16[1,512,512]{2,1,0:T(8,128)(2,1)} async-done(((bf16[4,512,512]{2,1,0:T(8,128)(2,1)}), bf16[1,512,512]{2,1,0:T(8,128)(2,1)}) %reduce-scatter.8.cloned.1.call-update) | async-done | bytes 524304 | tf_op jit(solution)/shard_map/reduce_scatter | solution.py:785
  502.3 36.8 %shard_map.195 = bf16[8,256,512]{2,1,0:T(8,128)(2,1)} custom-call(bf16[2,1024,512]{2,1,0:T(8,128)(2,1)} %get-tuple-element.56.refs_0_), custom_call_target="tpu_custom_call" | custom-call | tf_op jit(solution)/shard_map/pallas_call | solution.py:110
  539.1 4.2 convert_element_type.17
  543.3 51.4 %all-reduce = (f32[512]{0:T(512)}, f32[512]{0:T(512)}, f32[512,8]{0,1:T(8,128)}) all-reduce(f32[512]{0:T(512)S(1)} %bitcast.54, f32[512]{0:T(512)S(1)} %bitcast.53, f32[512,8]{0,1:T(8,128)S(1)} %bitcast.48), channel_id=1, replica_groups=mesh['wide'=8,'narrow'=4] {'wide','narrow'}, use_global_device_ids=true, to_apply=%region_1.2 | all-reduce | flops 5120 | bytes 40960 | tf_op jit(solution)/shard_map/psum | solution.py:796
  594.7 1.1 slice.8
  596.1 1.1 copy.65
  598.6 6.7 %convert_element_type.20 = f32[8,512,512]{2,1,0:T(8,128)} convert(bf16[8,512,512]{2,1,0:T(8,128)(2,1)} %all-gather.9.cloned.1.call-done) | non-fusion elementwise | flops 2097152 | bytes 12582912 | tf_op jit(solution)/shard_map/convert_element_type | solution.py:788
  605.3 31.9 %all-gather.11.cloned.1.call-done = bf16[8,512,512]{2,1,0:T(8,128)(2,1)} async-done(((bf16[1,512,512]{2,1,0:T(8,128)(2,1)}), bf16[8,512,512]{2,1,0:T(8,128)(2,1)}) %all-gather.11.cloned.1.call-update) | async-done | bytes 4194320 | tf_op jit(solution)/shard_map/all_gather | solution.py:786
  637.2 6.7 %convert_element_type.21 = f32[8,512,512]{2,1,0:T(8,128)} convert(bf16[8,512,512]{2,1,0:T(8,128)(2,1)} %all-gather.11.cloned.1.call-done) | non-fusion elementwise | flops 2097152 | bytes 12582912 | tf_op jit(solution)/shard_map/convert_element_type | solution.py:788
  644.0 1.3 copy.70
  (61 shorter events, 7.0 us)
Async XLA Ops:
  7.2 4.1 copy-start.3
  7.2 4.2 copy-start.2
  7.2 205.8 %all-gather.5.cloned.1.call-start = ((), (), s32[]{:S(2)}) async-start(), calls=%async_computation.3 | async-start | bytes 2621440 | tf_op jit(solution)/shard_map/all_gather | solution.py:700
  9.2 2.6 copy-start.7
  9.2 4.0 copy-start.4
  9.2 4.0 copy-start.5
  9.2 203.8 %all-gather.7.cloned.1.call-start = ((), (), s32[]{:S(2)}) async-start(), calls=%async_computation.4 | async-start | bytes 2621440 | tf_op jit(solution)/shard_map/all_gather | solution.py:703
  11.2 399.1 %reduce-scatter.4.cloned.1.call-start = ((), (), s32[]{:S(2)}) async-start(), calls=%async_computation.5 | async-start | bytes 2621440 | tf_op jit(solution)/shard_map/reduce_scatter | solution.py:792
  366.1 90.3 %reduce-scatter.6.cloned.1.call-start = ((), (), s32[]{:S(2)}) async-start(), calls=%async_computation.7 | async-start | bytes 2621440 | tf_op jit(solution)/shard_map/reduce_scatter | solution.py:785
  366.7 135.6 %reduce-scatter.8.cloned.1.call-start = ((), (), s32[]{:S(2)}) async-start(), calls=%async_computation.9 | async-start | bytes 2621440 | tf_op jit(solution)/shard_map/reduce_scatter | solution.py:785
  367.3 227.4 %all-reduce.3.cloned.1.call-start = ((), (), s32[]{:S(2)}) async-start(), calls=%async_computation.6 | async-start | bytes 1048576 | tf_op jit(solution)/shard_map/psum | solution.py:793
  410.3 188.2 %all-gather.9.cloned.1.call-start = ((), (), s32[]{:S(2)}) async-start(), calls=%async_computation.8 | async-start | bytes 4718592 | tf_op jit(solution)/shard_map/all_gather | solution.py:786
  456.4 180.8 %all-gather.11.cloned.1.call-start = ((), (), s32[]{:S(2)}) async-start(), calls=%async_computation.10 | async-start | bytes 4718592 | tf_op jit(solution)/shard_map/all_gather | solution.py:786
  539.1 4.2 copy-start.6
  539.1 4.2 copy-start.8
  539.1 4.2 copy-start.9
  594.7 2.5 copy-start
  605.3 38.6 %copy-start.1 = (bf16[8,256,512]{2,1,0:T(8,128)(2,1)S(1)}, bf16[8,256,512]{2,1,0:T(8,128)(2,1)}, u32[]{:S(2)}) copy-start(bf16[8,256,512]{2,1,0:T(8,128)(2,1)} %get-tuple-element.122) | copy-start | bytes 6291460
Sparse Core Ops, SparseCore 0:
  10.2 77.1 all-gather.4
  89.5 93.2 all-gather.6
  366.2 44.0 reduce-scatter.3
  413.1 43.1 reduce-scatter.5
  459.1 43.1 reduce-scatter.7
  505.5 52.2 all-reduce.2
  559.7 38.8 all-gather.8
  600.5 36.7 all-gather.10

commit v3 on v0

v3 whole, which is shorter than its diff:
```python
import functools

import jax
import jax.numpy as jnp
from jax import lax
from jax.experimental import pallas as pl
from jax.experimental.pallas import tpu as pltpu
from jax.sharding import PartitionSpec as P

MESH = pl.DeviceIdType.MESH
HEAD_DIM = 64
PAIR = 2 * HEAD_DIM
EPS = 1e-06
NEG = -1e30
bf16 = jnp.bfloat16
f32 = jnp.float32
VMEM_LIMIT = 60 << 20


def nn(a, b):
    return lax.dot_general(a, b, (((1,), (0,)), ((), ())), preferred_element_type=f32)


def nt(a, b):
    return lax.dot_general(a, b, (((1,), (1,)), ((), ())), preferred_element_type=f32)


def tn(a, b):
    return lax.dot_general(a, b, (((0,), (0,)), ((), ())), preferred_element_type=f32)


def whole(memory=pltpu.VMEM):
    return pl.BlockSpec(memory_space=memory)


def rows_of(first, count, size):
    return pl.ds(pl.multiple_of(first * size, size), count * size)


def peers(kind, sizes):
    narrow, wide, twins = sizes
    w, z = lax.axis_index("wide"), lax.axis_index("narrow")
    first = (w // twins) * twins
    if kind == "narrow":
        return z, narrow, lambda j: (w, j)
    if kind == "wide":
        return w, wide, lambda j: (j, z)
    if kind == "twin":
        return w - first, twins, lambda j: (first + j, z)
    if kind == "row":
        return w // twins, wide // twins, lambda j: (j * twins + w - first, z)
    if kind == "column":
        return (
            z * twins + w - first,
            narrow * twins,
            lambda j: (first + lax.rem(j, twins), j // twins),
        )
    return w * narrow + z, wide * narrow, lambda j: (j // narrow, lax.rem(j, narrow))


def group_size(kind, sizes):
    narrow, wide, twins = sizes
    return {
        "narrow": narrow,
        "wide": wide,
        "twin": twins,
        "row": wide // twins,
        "column": narrow * twins,
        "all": wide * narrow,
    }[kind]


def plan(kinds, sizes):
    bases, used = {}, 0
    for name, kind in kinds.items():
        bases[name] = used
        used += group_size(kind, sizes)
    return bases, used


class Exchange:
    def __init__(self, kind, sizes, source_at, target_at, sems, base, own=None):
        self.me, self.total, self.place = peers(kind, sizes)
        self.source_at, self.target_at = source_at, target_at
        (self.send, self.recv, self.local), self.base, self.own = sems, base, own

    def copy_of(self, k):
        j = lax.rem(self.me + k, self.total)
        return pltpu.make_async_remote_copy(
            src_ref=self.source_at(j),
            dst_ref=self.target_at(self.me),
            send_sem=self.send.at[self.base + k],
            recv_sem=self.recv.at[self.base + k],
            device_id=self.place(j),
            device_id_type=MESH,
        )

    def each(self, action):
        def step(k, carry):
            action(self.copy_of(k))
            return carry

        lax.fori_loop(1, self.total, step, 0)

    def kept(self):
        return pltpu.make_async_copy(
            self.source_at(self.me), self.target_at(self.me), self.local.at[self.own]
        )

    def start(self):
        self.each(lambda c: c.start())
        if self.own is not None:
            self.kept().start()

    def wait_recv(self):
        self.each(lambda c: c.wait_recv())
        if self.own is not None:
            self.kept().wait()

    def wait_send(self):
        self.each(lambda c: c.wait_send())


def greet(sizes):
    barrier = pltpu.get_barrier_semaphore()
    me, total, place = peers("all", sizes)

    def step(k, carry):
        pl.semaphore_signal(
            barrier, inc=1, device_id=place(lax.rem(me + k, total)), device_id_type=MESH
        )
        return carry

    lax.fori_loop(1, total, step, 0)
    pl.semaphore_wait(barrier, total - 1)


def unit_of(values):
    scaling = lax.rsqrt(jnp.mean(values * values, axis=-1, keepdims=True) + EPS)
    return values * scaling, scaling


def unit_back(grad_rows, unit_rows, scaling, gain):
    grad_unit = grad_rows * gain
    inner = jnp.mean(grad_unit * unit_rows, axis=-1, keepdims=True)
    return scaling * (grad_unit - unit_rows * inner)


def wall_of(wall_ref, n):
    part = wall_ref[n]
    return part.reshape(-1, part.shape[-1])


def attend_pairs(
    block, s, low, high, normed, start_ref, wall_ref, qkv_ref, att_ref, lse_acc, stored
):
    length = normed.shape[0]
    lane = lax.broadcasted_iota(jnp.int32, (block, PAIR), 1)

    def one_pair(n, carry):
        proj = nn(normed[...], wall_of(wall_ref, n)[:, : 3 * PAIR]).astype(bf16)
        qkv_ref[s, n] = proj
        keys, vals = proj[:, PAIR : 2 * PAIR], proj[:, 2 * PAIR :]
        for i in range(length // block):
            rows = slice(i * block, (i + 1) * block)
            end = (i + 1) * block
            query = proj[rows, :PAIR] * jnp.asarray(HEAD_DIM**-0.5, bf16)
            key_at = lax.broadcasted_iota(jnp.int32, (block, end), 1)
            row_at = i * block + lax.broadcasted_iota(jnp.int32, (block, end), 0)
            allowed = (key_at >= start_ref[s, rows, :]) & (key_at <= row_at)
            got = []
            for j in range(2):
                own = (lane // HEAD_DIM) == j
                score = nt(jnp.where(own, query, jnp.zeros_like(query)), keys[:end])
                score = jnp.where(allowed, score, NEG)
                peak = jnp.max(score, axis=1, keepdims=True)
                expo = jnp.exp(score - peak)
                total = jnp.sum(expo, axis=1, keepdims=True)
                got.append(nn(expo.astype(bf16), vals[:end]) / total)
                lse_acc[rows, :] = jnp.where(
                    lane == 2 * n + j, peak + jnp.log(total), lse_acc[rows, :]
                )
            att_ref[s, n, rows, :] = jnp.where(lane < HEAD_DIM, got[0], got[1]).astype(bf16)
        stored(s, n)
        return carry

    lax.fori_loop(low, high, one_pair, 0)


def forward_kinds(seqs):
    kinds = {"wall": "narrow", "wall_row": "row", "wall_twin": "twin", "cot": "wide"}
    for t in range(2):
        kinds[f"weight{t}"], kinds[f"weight_row{t}"] = "narrow", "row"
    for s in range(seqs):
        kinds[f"x{s}"], kinds[f"hid{s}"] = "narrow", "all"
    return kinds


def forward_body(
    sizes,
    block,
    bases,
    inputs_ref,
    cot_ref,
    wall_own_ref,
    up_ref,
    down_ref,
    start_ref,
    gain_ref,
    xmix_ref,
    gmix_ref,
    weight_ref,
    x_out,
    wall_out,
    qkv_out,
    att_out,
    lse_ref,
    x_ref,
    wall_ref,
    qkv_ref,
    att_ref,
    hid_ref,
    normed_ref,
    lse_acc,
    send,
    recv,
    local,
    out_sem,
):
    narrow, wide, twins = sizes
    w, z = lax.axis_index("wide"), lax.axis_index("narrow")
    seqs, length, features = x_ref.shape
    seq_dev, local_len, _ = inputs_ref.shape
    pos_dev = local_len // wide
    pairs = wall_ref.shape[0]
    row, twin = w // twins, lax.rem(w, twins)
    wall_rows = features // wide
    weight_rows = features // (wide // twins)
    sems = (send, recv, local)

    def exchange(name, kind, source_at, target_at, own=None):
        return Exchange(kind, sizes, source_at, target_at, sems, bases[name], own)

    greet(sizes)
    wall = exchange(
        "wall",
        "narrow",
        lambda j: wall_own_ref.at[rows_of(w, 1, wall_rows)],
        lambda j: wall_ref.at[j, row, twin],
        0,
    )
    wall_row = exchange(
        "wall_row",
        "row",
        lambda j: wall_ref.at[:, row, twin],
        lambda j: wall_ref.at[:, j, twin],
    )
    wall_twin = exchange(
        "wall_twin", "twin", lambda j: wall_ref.at[:, :, twin], lambda j: wall_ref.at[:, :, j]
    )
    cot = exchange(
        "cot",
        "wide",
        lambda j: cot_ref.at[:, rows_of(j, 1, pos_dev)],
        lambda j: gmix_ref.at[pl.ds(j * seq_dev, seq_dev)],
        1,
    )
    mine = rows_of(row, 1, weight_rows)
    weight = [
        exchange(
            f"weight{t}",
            "narrow",
            lambda j, ref=ref: ref.at[j * twins + twin, mine],
            lambda j, t=t: weight_ref.at[t, j, mine],
            2 + t,
        )
        for t, ref in enumerate((up_ref, down_ref))
    ]
    weight_row = [
        exchange(
            f"weight_row{t}",
            "row",
            lambda j, t=t: weight_ref.at[t, :, mine],
            lambda j, t=t: weight_ref.at[t, :, rows_of(j, 1, weight_rows)],
        )
        for t in range(2)
    ]
    x_in = [
        exchange(
            f"x{s}",
            "narrow",
            lambda j, s=s: inputs_ref.at[j * seqs + s],
            lambda j, s=s: x_ref.at[s, rows_of(j, 1, local_len)],
            4 + s,
        )
        for s in range(seqs)
    ]
    hid = [
        exchange(
            f"hid{s}",
            "all",
            lambda j, s=s: hid_ref.at[
                s, rows_of(lax.rem(j, narrow) * wide + j // narrow, 1, pos_dev)
            ],
            lambda j, s=s: xmix_ref.at[j * seqs + s],
            4 + seqs + s,
        )
        for s in range(seqs)
    ]

    def kept(s, n):
        return (
            pltpu.make_async_copy(qkv_ref.at[s, n], qkv_out.at[s, n], out_sem.at[s, 2 * n]),
            pltpu.make_async_copy(att_ref.at[s, n], att_out.at[s, n], out_sem.at[s, 2 * n + 1]),
        )

    def stored(s, n):
        for c in kept(s, n):
            c.start()

    wall_keep = pltpu.make_async_copy(wall_ref, wall_out, out_sem.at[0, 2 * pairs])
    x_keep = [
        pltpu.make_async_copy(x_ref.at[s], x_out.at[s], out_sem.at[s, 2 * pairs + 1])
        for s in range(seqs)
    ]

    wall.start()
    x_in[0].start()
    wall.wait_recv()
    wall_row.start()
    wall_row.wait_recv()
    wall_twin.start()
    cot.start()
    wall_twin.wait_recv()
    x_in[0].wait_recv()
    weight[0].start()
    weight[1].start()
    wall_keep.start()
    for s in range(seqs):
        if s > 0:
            x_in[s].wait_recv()
        x_keep[s].start()
        normed_ref[...] = (unit_of(x_ref[s].astype(f32))[0] * gain_ref[...]).astype(bf16)

        def pairs_of(low, high, s=s):
            attend_pairs(
                block, s, low, high, normed_ref, start_ref, wall_ref, qkv_ref, att_ref, lse_acc, stored
            )

        pairs_of(0, pairs // 2)
        if s + 1 < seqs:
            x_in[s + 1].start()
        pairs_of(pairs // 2, pairs)
        hidden = x_ref[s].astype(f32)
        for n in range(pairs):
            hidden = hidden + nt(att_ref[s, n], wall_of(wall_ref, n)[:, 3 * PAIR :])
        hid_ref[s] = hidden.astype(bf16)
        hid[s].start()
        lse_ref[s] = jnp.transpose(lse_acc[...])[: 2 * pairs]
        if s == 0:
            for t in range(2):
                weight[t].wait_recv()
                weight_row[t].start()
    for e in (wall, wall_row, wall_twin, cot, *weight, *weight_row, *x_in):
        e.wait_send()
    cot.wait_recv()
    for t in range(2):
        weight_row[t].wait_recv()
    wall_keep.wait()
    for s in range(seqs):
        x_keep[s].wait()

        def settle(n, carry, s=s):
            for c in kept(s, n):
                c.wait()
            return carry

        lax.fori_loop(0, pairs, settle, 0)
    for s in range(seqs):
        hid[s].wait_recv()
        hid[s].wait_send()


def forward(inputs, cot, wall_own, up, down, start_col, gain, sizes):
    narrow, wide, twins = sizes
    seq_dev, local_len, features = inputs.shape
    seqs, length, pairs = seq_dev // narrow, local_len * narrow, narrow
    pos_dev = local_len // wide
    wall_shape = (pairs, wide // twins, twins, features // wide, wall_own.shape[1])
    bases, used = plan(forward_kinds(seqs), sizes)
    dma = pltpu.SemaphoreType.DMA
    qkv_shape = (seqs, pairs, length, 3 * PAIR)
    att_shape = (seqs, pairs, length, PAIR)
    mix_shape = (seq_dev * wide, pos_dev, features)
    return pl.pallas_call(
        functools.partial(forward_body, sizes, min(256, length), bases),
        out_shape=[
            jax.ShapeDtypeStruct(mix_shape, bf16),
            jax.ShapeDtypeStruct(mix_shape, bf16),
            jax.ShapeDtypeStruct((2, narrow) + up.shape[1:], bf16),
            jax.ShapeDtypeStruct((seqs, length, features), bf16),
            jax.ShapeDtypeStruct(wall_shape, bf16),
            jax.ShapeDtypeStruct(qkv_shape, bf16),
            jax.ShapeDtypeStruct(att_shape, bf16),
            jax.ShapeDtypeStruct((seqs, 2 * pairs, length), f32),
        ],
        in_specs=[whole(pl.ANY)] * 5 + [whole()] * 2,
        out_specs=[whole(pl.ANY)] * 7 + [whole()],
        scratch_shapes=[
            pltpu.VMEM((seqs, length, features), bf16),
            pltpu.VMEM(wall_shape, bf16),
            pltpu.VMEM(qkv_shape, bf16),
            pltpu.VMEM(att_shape, bf16),
            pltpu.VMEM((seqs, length, features), bf16),
            pltpu.VMEM((length, features), bf16),
            pltpu.VMEM((length, PAIR), f32),
            dma((used,)),
            dma((used,)),
            dma((4 + 2 * seqs,)),
            dma((seqs, 2 * pairs + 2)),
        ],
        compiler_params=pltpu.CompilerParams(
            collective_id=1, has_side_effects=True, vmem_limit_bytes=VMEM_LIMIT
        ),
    )(inputs, cot, wall_own, up, down, start_col, gain)


def mix_forward(experts, cells, x_ref, key_ref, gain_ref, router_ref, normed_ref, weight_ref, low_ref, logit_ref):
    tokens = x_ref.shape[0]
    chunk = min(512, tokens)

    def norm_rows(c, carry):
        rows = rows_of(c, 1, chunk)
        unit = unit_of(x_ref[rows, :].astype(f32))[0]
        normed_ref[rows, :] = (unit * gain_ref[...]).astype(bf16)
        return carry

    lax.fori_loop(0, tokens // chunk, norm_rows, 0)
    logit_ref[...] = nt(router_ref[...], normed_ref[...])

    def one_expert(e, carry):
        cell = lax.broadcasted_iota(jnp.int32, (cells, tokens), 0)
        score = jnp.where(cell == key_ref[...], logit_ref[pl.ds(e, 1), :], NEG)
        expo = jnp.exp(score - jnp.max(score, axis=1, keepdims=True))
        weights = expo / jnp.sum(expo, axis=1, keepdims=True)
        rows = rows_of(e, 1, cells)
        weight_ref[rows, :] = weights
        low_ref[rows, :] = weights.astype(bf16)
        return carry

    lax.fori_loop(0, experts, one_expert, 0)


def gelu_parts(pre):
    square = pre * pre
    tanh = jnp.tanh(0.7978845608028654 * (pre + 0.044715 * pre * square))
    act = 0.5 * pre * (1.0 + tanh)
    slope = 0.5 * (1.0 + tanh) + 0.5 * pre * (1.0 - tanh * tanh) * (
        0.7978845608028654 * (1.0 + 3 * 0.044715 * square)
    )
    return act, slope


def mix_weights_back(experts, cells, weight_ref, gw_ref, gl_ref):
    def one_expert(e, carry):
        rows = rows_of(e, 1, cells)
        weights, grads = weight_ref[rows, :], gw_ref[rows, :]
        inner = jnp.sum(weights * grads, axis=1, keepdims=True)
        gl_ref[pl.ds(e, 1), :] = jnp.sum(weights * (grads - inner), axis=0, keepdims=True)
        return carry

    lax.fori_loop(0, experts, one_expert, 0)


def attend_back_pairs(
    block, s, last, low, high, start_ref, lse_ref, x_n, x_nt, dh_ref, dh_t, wall_ref, qkv_ref, att_ref, dq_acc, dproj_ref, gn_acc, gw_acc, finished
):
    length = x_n.shape[0]
    lane = lax.broadcasted_iota(jnp.int32, (length, PAIR), 1)
    scale = jnp.asarray(HEAD_DIM**-0.5, bf16)

    def one_pair(n, carry):
        wall = wall_of(wall_ref, n)
        d_att = nn(dh_ref[s], wall[:, 3 * PAIR :]).astype(bf16)
        att = att_ref[s, n]
        g_out = nn(dh_t[...], att)
        prod = (d_att.astype(f32) * att.astype(f32)).astype(bf16)
        head_row = lax.broadcasted_iota(jnp.int32, (8, PAIR), 0)
        head_lane = lax.broadcasted_iota(jnp.int32, (8, PAIR), 1) // HEAD_DIM
        inner = nt((head_row == head_lane).astype(bf16), prod)
        query = qkv_ref[s, n, :, :PAIR] * scale
        keys, vals = qkv_ref[s, n, :, PAIR : 2 * PAIR], qkv_ref[s, n, :, 2 * PAIR :]
        zero = jnp.zeros_like(query)
        own = [(lane // HEAD_DIM) == j for j in range(2)]
        q_own = [jnp.where(o, query, zero) for o in own]
        k_own = [jnp.where(o, keys, zero) for o in own]
        d_own = [jnp.where(o, d_att, zero) for o in own]
        lse_own = [lse_ref[s, pl.ds(2 * n + j, 1), :] for j in range(2)]
        dq_acc[...] = jnp.zeros_like(dq_acc)
        for i in range(length // block):
            rows, first = slice(i * block, (i + 1) * block), i * block
            shape = (block, length - first)
            key_at = first + lax.broadcasted_iota(jnp.int32, shape, 0)
            row_at = first + lax.broadcasted_iota(jnp.int32, shape, 1)
            allowed = (key_at >= start_ref[s, :, first:]) & (key_at <= row_at)
            dk = dv = None
            for j in range(2):
                score = nt(keys[rows], q_own[j][first:])
                prob = jnp.where(allowed, jnp.exp(score - lse_own[j][:, first:]), 0.0)
                d_prob = nt(vals[rows], d_own[j][first:])
                d_score = (prob * (d_prob - inner[j : j + 1, first:])).astype(bf16)
                dv_part = nn(prob.astype(bf16), d_own[j][first:])
                dk_part = nn(d_score, q_own[j][first:])
                dv = dv_part if dv is None else dv + dv_part
                dk = dk_part if dk is None else dk + dk_part
                dq_acc[first:, :] += tn(d_score, k_own[j][rows])
            dproj_ref[rows, PAIR : 2 * PAIR] = dk.astype(bf16)
            dproj_ref[rows, 2 * PAIR :] = dv.astype(bf16)
        dproj_ref[:, :PAIR] = (dq_acc[...] * HEAD_DIM**-0.5).astype(bf16)
        d_proj = dproj_ref[...]
        gn_acc[...] += nt(d_proj, wall[:, : 3 * PAIR])
        g_in = nn(x_nt[...], d_proj)
        if s == 0:
            gw_acc[n, :, : 3 * PAIR] = g_in
            gw_acc[n, :, 3 * PAIR :] = g_out
        else:
            gw_acc[n, :, : 3 * PAIR] += g_in
            gw_acc[n, :, 3 * PAIR :] += g_out
        if last:
            finished(n)
        return carry

    lax.fori_loop(low, high, one_pair, 0)


def back_kinds(seqs, pairs):
    kinds = {name: "column" for name in ("mixed", "gexp", "eo", "gm")}
    kinds["out"] = "wide"
    for t in range(2):
        kinds[f"sum_row{t}"], kinds[f"sum_z{t}"] = "row", "narrow"
        kinds[f"full_row{t}"], kinds[f"full_twin{t}"] = "row", "twin"
    for s in range(seqs):
        kinds[f"dh{s}"], kinds[f"gx{s}"] = "all", "narrow"
    for n in range(pairs):
        kinds[f"wall_twin{n}"] = "twin"
    kinds["wall_row"], kinds["wall_z"], kinds["wall_full"] = "row", "narrow", "wide"
    kinds["small_w"], kinds["small_z"] = "wide", "narrow"
    return kinds


def backward_body(
    sizes,
    block,
    bases,
    xmix_in,
    gmix_in,
    weight_in,
    x_in,
    wall_in,
    qkv_in,
    att_in,
    key_ref,
    start_ref,
    lse_ref,
    gain_one,
    gain_two,
    router_ref,
    out_home,
    gx_home,
    full_ref,
    wall_out,
    small_out,
    mixed_src,
    gexp_src,
    eo_src,
    gm_src,
    mixed_land,
    gexp_land,
    eo_land,
    gm_land,
    grad_src,
    sum_land,
    sum_src,
    gh_ref,
    out_ref,
    dh_ref,
    gx_ref,
    gw_src,
    gw_twin,
    gw_half,
    gw_row,
    gw_z_src,
    gw_z,
    gw_last,
    small_ref,
    small_w,
    small_mid,
    small_z,
    send,
    recv,
    local,
    load_sem,
):
    narrow, wide, twins = sizes
    w, z = lax.axis_index("wide"), lax.axis_index("narrow")
    row, twin = w // twins, lax.rem(w, twins)
    row_count = wide // twins
    seqs, length, features = dh_ref.shape
    seq_total, pos_dev, _ = gh_ref.shape
    tokens = seq_total * pos_dev
    seq_dev, local_len, _ = out_home.shape
    experts = router_ref.shape[0]
    cells = mixed_src.shape[0] // experts
    pairs = gw_src.shape[0]
    part_rows = sum_src.shape[2]
    wall_rows = gw_last.shape[0]
    mine = rows_of(row, 1, part_rows)
    sems = (send, recv, local)
    owns = iter(range(local.shape[0]))

    def exchange(name, kind, source_at, target_at, own=False):
        return Exchange(
            kind, sizes, source_at, target_at, sems, bases[name], next(owns) if own else None
        )

    def column(name, source, target):
        return exchange(
            name,
            "column",
            lambda j: source.at[rows_of(j, 1, cells)],
            lambda j: target.at[rows_of(j, 1, cells)],
            True,
        )

    mixed_x = column("mixed", mixed_src, mixed_land)
    gexp_x = column("gexp", gexp_src, gexp_land)
    eo_x = column("eo", eo_src, eo_land)
    gm_x = column("gm", gm_src, gm_land)
    out_x = exchange(
        "out",
        "wide",
        lambda j: out_ref.at[pl.ds(j * seq_dev, seq_dev)],
        lambda j: out_home.at[:, rows_of(j, 1, pos_dev)],
        True,
    )
    sum_row = [
        exchange(
            f"sum_row{t}",
            "row",
            lambda j, t=t: grad_src.at[t, :, rows_of(j, 1, part_rows)],
            lambda j, t=t: sum_land.at[j, t],
        )
        for t in range(2)
    ]
    sum_z = [
        exchange(
            f"sum_z{t}",
            "narrow",
            lambda j, t=t: sum_src.at[t, j],
            lambda j, t=t: full_ref.at[t, j, twin, mine],
            True,
        )
        for t in range(2)
    ]
    full_row = [
        exchange(
            f"full_row{t}",
            "row",
            lambda j, t=t: full_ref.at[t, :, twin, mine],
            lambda j, t=t: full_ref.at[t, :, twin, rows_of(j, 1, part_rows)],
        )
        for t in range(2)
    ]
    full_twin = [
        exchange(
            f"full_twin{t}",
            "twin",
            lambda j, t=t: full_ref.at[t, :, twin],
            lambda j, t=t: full_ref.at[t, :, j],
        )
        for t in range(2)
    ]
    dh_x = [
        exchange(
            f"dh{s}",
            "all",
            lambda j, s=s: gh_ref.at[j * seqs + s],
            lambda j, s=s: dh_ref.at[
                s, rows_of(lax.rem(j, narrow) * wide + j // narrow, 1, pos_dev)
            ],
            True,
        )
        for s in range(seqs)
    ]
    gx_x = [
        exchange(
            f"gx{s}",
            "narrow",
            lambda j, s=s: gx_ref.at[s, rows_of(j, 1, local_len)],
            lambda j, s=s: gx_home.at[j * seqs + s],
            True,
        )
        for s in range(seqs)
    ]

    def wall_twin(n):
        e = exchange(
            "wall_twin0",
            "twin",
            lambda j: gw_src.at[n, :, j],
            lambda j: gw_twin.at[j, n],
        )
        e.base = bases["wall_twin0"] + n * twins
        return e

    wall_row = exchange(
        "wall_row", "row", lambda j: gw_half.at[:, j], lambda j: gw_row.at[j]
    )
    wall_z = exchange("wall_z", "narrow", lambda j: gw_z_src.at[j], lambda j: gw_z.at[j])
    wall_full = exchange(
        "wall_full",
        "wide",
        lambda j: gw_last,
        lambda j: wall_out.at[rows_of(j, 1, wall_rows)],
        True,
    )
    small_wide = exchange("small_w", "wide", lambda j: small_ref, lambda j: small_w.at[j])
    small_narrow = exchange("small_z", "narrow", lambda j: small_mid, lambda j: small_z.at[j])

    greet(sizes)

    def mixture(x_ref, g_ref, normed_ref, weight_ref, low_ref, low_t, logit_ref):
        x_load = pltpu.make_async_copy(xmix_in, x_ref, load_sem.at[0])
        g_load = pltpu.make_async_copy(gmix_in, g_ref, load_sem.at[1])
        x_load.start()
        g_load.start()

        def experts_of(up_down, act_ref, slope_ref, pre_ref):
            w_load = pltpu.make_async_copy(weight_in, up_down, load_sem.at[2])
            w_load.start()
            x_load.wait()
            mix_forward(
                experts, cells, x_ref, key_ref, gain_two, router_ref, normed_ref, weight_ref, low_ref, logit_ref
            )
            mixed_src[...] = nn(low_ref[...], normed_ref[...]).astype(bf16)
            mixed_x.start()
            g_load.wait()
            gexp_src[...] = nn(low_ref[...], g_ref[...]).astype(bf16)
            gexp_x.start()
            low_t[...] = jnp.transpose(low_ref[...])
            w_load.wait()
            mixed_x.wait_recv()
            rows = mixed_land[...]
            total = None
            for h in range(narrow):
                act, slope = gelu_parts(nn(rows, up_down[0, h]))
                act_ref[h] = act.astype(bf16)
                slope_ref[h] = slope.astype(bf16)
                part = nn(act_ref[h], up_down[1, h])
                total = part if total is None else total + part
            eo_src[...] = total.astype(bf16)
            eo_x.start()
            gexp_x.wait_recv()
            total = None
            for h in range(narrow):
                pre = nt(gexp_land[...], up_down[1, h]) * slope_ref[h].astype(f32)
                pre_ref[h] = pre.astype(bf16)
                part = nt(pre_ref[h], up_down[0, h])
                total = part if total is None else total + part
            gm_src[...] = total.astype(bf16)
            gm_x.start()
            rows_t = jnp.transpose(rows)
            for h in range(narrow):
                grad_src[0, h] = nn(rows_t, pre_ref[h]).astype(bf16)
            sum_row[0].start()
            for h in range(narrow):
                grad_src[1, h] = tn(act_ref[h], gexp_land[...]).astype(bf16)
            sum_row[1].start()

        part_shape = weight_in.shape[1:]
        pl.run_scoped(
            experts_of,
            pltpu.VMEM(weight_in.shape, bf16),
            pltpu.VMEM(part_shape, bf16),
            pltpu.VMEM(part_shape, bf16),
            pltpu.VMEM(part_shape, bf16),
        )

        def come_back(gw_ref, gl_ref):
            chunk = min(512, tokens)
            seq_chunk = chunk // pos_dev
            eo_x.wait_recv()

            def out_rows(c, carry):
                rows = rows_of(c, 1, chunk)
                got = x_ref[rows, :].astype(f32) + nn(low_t[rows, :], eo_land[...])
                out_ref[pl.ds(c * seq_chunk, seq_chunk)] = got.astype(bf16).reshape(
                    seq_chunk, pos_dev, features
                )
                return carry

            lax.fori_loop(0, tokens // chunk, out_rows, 0)
            gw_ref[...] = nt(eo_land[...], g_ref[...])
            gm_x.wait_recv()
            gw_ref[...] += nt(gm_land[...], normed_ref[...])
            mix_weights_back(experts, cells, weight_ref, gw_ref, gl_ref)
            g_logit = gl_ref[...].astype(bf16)
            small_ref[:experts, :] = nn(g_logit, normed_ref[...])
            small_ref[experts:, :] = jnp.zeros((small_ref.shape[0] - experts, features), f32)

            def back_rows(c, carry):
                rows = rows_of(c, 1, chunk)
                unit, scaling = unit_of(x_ref[rows, :].astype(f32))
                g_l = gl_ref[:, rows].astype(bf16)
                g_normed = nn(low_t[rows, :], gm_land[...]) + tn(g_l, router_ref[...])
                small_ref[experts : experts + 1, :] += jnp.sum(
                    g_normed * unit, axis=0, keepdims=True
                )
                got = g_ref[rows, :].astype(f32) + unit_back(g_normed, unit, scaling, gain_two[...])
                gh_ref[pl.ds(c * seq_chunk, seq_chunk)] = got.astype(bf16).reshape(
                    seq_chunk, pos_dev, features
                )
                return carry

            lax.fori_loop(0, tokens // chunk, back_rows, 0)

        pl.run_scoped(
            come_back,
            pltpu.VMEM((experts * cells, tokens), f32),
            pltpu.VMEM((experts, tokens), f32),
        )

    pl.run_scoped(
        mixture,
        pltpu.VMEM((tokens, features), bf16),
        pltpu.VMEM((tokens, features), bf16),
        pltpu.VMEM((tokens, features), bf16),
        pltpu.VMEM((experts * cells, tokens), f32),
        pltpu.VMEM((experts * cells, tokens), bf16),
        pltpu.VMEM((tokens, experts * cells), bf16),
        pltpu.VMEM((experts, tokens), f32),
    )
    dh_x[0].start()
    out_x.start()

    def sum_rows():
        for t in range(2):
            sum_row[t].wait_recv()
            for h in range(narrow):
                total = grad_src[t, h, mine, :].astype(f32)
                for k in range(1, row_count):
                    total = total + sum_land[lax.rem(row + k, row_count), t, h].astype(f32)
                sum_src[t, h] = total.astype(bf16)
            sum_z[t].start()

    def attention(x_ref, wall_ref, qkv_ref, att_ref, x_n, x_nt, dh_t, gn_acc, gw_acc, dq_acc, dproj_ref):
        loads = [
            pltpu.make_async_copy(source, target, load_sem.at[3 + i])
            for i, (source, target) in enumerate(
                ((x_in, x_ref), (wall_in, wall_ref), (qkv_in, qkv_ref), (att_in, att_ref))
            )
        ]
        for c in loads:
            c.start()
        for c in loads:
            c.wait()

        def finished(n):
            part = gw_acc[n].astype(bf16)
            gw_src[n] = part.reshape(gw_src.shape[1:])
            wall_twin(n).start()

        for s in range(seqs):
            unit, _ = unit_of(x_ref[s].astype(f32))
            x_n[...] = (unit * gain_one[...]).astype(bf16)
            x_nt[...] = jnp.transpose(x_n[...])
            gn_acc[...] = jnp.zeros_like(gn_acc)
            dh_x[s].wait_recv()
            if s + 1 < seqs:
                dh_x[s + 1].start()
            dh_t[...] = jnp.transpose(dh_ref[s])

            def pairs_of(low, high, s=s):
                attend_back_pairs(
                    block, s, s == seqs - 1, low, high, start_ref, lse_ref, x_n, x_nt, dh_ref, dh_t, wall_ref, qkv_ref, att_ref, dq_acc, dproj_ref, gn_acc, gw_acc, finished
                )

            pairs_of(0, pairs // 2)
            if s == 0:
                sum_rows()
            elif s == 1:
                for t in range(2):
                    sum_z[t].wait_recv()
                    full_row[t].start()
            pairs_of(pairs // 2, pairs)
            unit, scaling = unit_of(x_ref[s].astype(f32))
            grad = gn_acc[...]
            small_ref[experts + 1 : experts + 2, :] += jnp.sum(grad * unit, axis=0, keepdims=True)
            got = dh_ref[s].astype(f32) + unit_back(grad, unit, scaling, gain_one[...])
            gx_ref[s] = got.astype(bf16)
            gx_x[s].start()

    pl.run_scoped(
        attention,
        pltpu.VMEM(x_in.shape, bf16),
        pltpu.VMEM(wall_in.shape, bf16),
        pltpu.VMEM(qkv_in.shape, bf16),
        pltpu.VMEM(att_in.shape, bf16),
        pltpu.VMEM((length, features), bf16),
        pltpu.VMEM((features, length), bf16),
        pltpu.VMEM((features, length), bf16),
        pltpu.VMEM((length, features), f32),
        pltpu.VMEM((pairs, features, 4 * PAIR), f32),
        pltpu.VMEM((length, PAIR), f32),
        pltpu.VMEM((length, 3 * PAIR), bf16),
    )
    small_wide.start()
    for n in range(pairs):
        wall_twin(n).wait_recv()
        total = gw_src[n, :, twin].astype(f32)
        for k in range(1, twins):
            total = total + gw_twin[lax.rem(twin + k, twins), n].astype(f32)
        gw_half[n] = total.astype(bf16)
    wall_row.start()
    small_wide.wait_recv()
    small_w[w] = small_ref[...]
    total = small_w[0]
    for j in range(1, wide):
        total = total + small_w[j]
    small_mid[...] = total
    small_narrow.start()
    wall_row.wait_recv()
    total = gw_half[:, row].astype(f32)
    for k in range(1, row_count):
        total = total + gw_row[lax.rem(row + k, row_count)].astype(f32)
    gw_z_src[...] = total.astype(bf16)
    wall_z.start()
    small_narrow.wait_recv()
    small_z[z] = small_mid[...]
    total = small_z[0]
    for j in range(1, narrow):
        total = total + small_z[j]
    small_out[...] = total
    wall_z.wait_recv()
    total = gw_z_src[z].astype(f32)
    for k in range(1, narrow):
        total = total + gw_z[lax.rem(z + k, narrow)].astype(f32)
    gw_last[...] = total.astype(bf16)
    wall_full.start()
    for t in range(2):
        full_row[t].wait_recv()
        full_twin[t].start()
    for e in (mixed_x, gexp_x, eo_x, gm_x, out_x, *sum_row, *sum_z, *dh_x):
        e.wait_send()
    for n in range(pairs):
        wall_twin(n).wait_send()
    for e in (wall_row, wall_z, small_wide, small_narrow, *full_row):
        e.wait_send()
    out_x.wait_recv()
    for e in (*gx_x, wall_full, *full_twin):
        e.wait_recv()
        e.wait_send()


def backward(x_mix, g_mix, weights, x_seq, wall, qkv, att, key_row, start_row, lse, gain_one, gain_two, router, home, sizes):
    narrow, wide, twins = sizes
    seq_total, pos_dev, features = x_mix.shape
    seqs, length, _ = x_seq.shape
    pairs, experts = narrow, router.shape[0]
    row_count = wide // twins
    tokens = seq_total * pos_dev
    _, _, hidden_rows, columns = weights.shape
    part_rows = hidden_rows // row_count
    wall_rows = features // wide
    cells = pos_dev * key_row[1]
    bases, used = plan(back_kinds(seqs, pairs), sizes)
    dma = pltpu.SemaphoreType.DMA
    rows = (experts * cells, features)
    vm = pltpu.VMEM
    return pl.pallas_call(
        functools.partial(backward_body, sizes, min(256, length), bases),
        out_shape=[
            jax.ShapeDtypeStruct(home, bf16),
            jax.ShapeDtypeStruct(home, bf16),
            jax.ShapeDtypeStruct((2, narrow, twins, hidden_rows, columns), bf16),
            jax.ShapeDtypeStruct((features, 4 * PAIR), bf16),
            jax.ShapeDtypeStruct((2 * experts, features), f32),
        ],
        in_specs=[whole(pl.ANY)] * 7 + [whole()] * 6,
        out_specs=[whole(pl.ANY)] * 4 + [whole()],
        scratch_shapes=[vm(rows, bf16)] * 8
        + [
            vm((2, narrow, hidden_rows, columns), bf16),
            vm((row_count, 2, narrow, part_rows, columns), bf16),
            vm((2, narrow, part_rows, columns), bf16),
            vm(x_mix.shape, bf16),
            vm(x_mix.shape, bf16),
            vm(x_seq.shape, bf16),
            vm(x_seq.shape, bf16),
            vm((pairs, row_count, twins, wall_rows, 4 * PAIR), bf16),
            vm((twins, pairs, row_count, wall_rows, 4 * PAIR), bf16),
            vm((pairs, row_count, wall_rows, 4 * PAIR), bf16),
            vm((row_count, pairs, wall_rows, 4 * PAIR), bf16),
            vm((pairs, wall_rows, 4 * PAIR), bf16),
            vm((narrow, wall_rows, 4 * PAIR), bf16),
            vm((wall_rows, 4 * PAIR), bf16),
            vm((2 * experts, features), f32),
            vm((wide, 2 * experts, features), f32),
            vm((2 * experts, features), f32),
            vm((narrow, 2 * experts, features), f32),
            dma((used,)),
            dma((used,)),
            dma((8 + 2 * seqs,)),
            dma((7,)),
        ],
        compiler_params=pltpu.CompilerParams(
            collective_id=2, has_side_effects=True, vmem_limit_bytes=VMEM_LIMIT
        ),
    )(
        x_mix.reshape(tokens, features),
        g_mix.reshape(tokens, features),
        weights,
        x_seq,
        wall,
        qkv,
        att,
        key_row[0],
        start_row,
        lse,
        gain_one,
        gain_two,
        router,
    )


def per_device(
    inputs,
    positions,
    members_index,
    members_mask,
    gain_attn,
    input_projection_weight,
    output_projection_weight,
    gain_mixer,
    weight_router,
    weight_up,
    weight_down,
    cotangent,
):
    narrow, wide = lax.axis_size("narrow"), lax.axis_size("wide")
    w, z = lax.axis_index("wide"), lax.axis_index("narrow")
    seq_dev, local_len, features = inputs.shape
    length = positions.shape[1]
    groups = members_index.shape[1]
    experts = weight_up.shape[0]
    own_seqs = seq_dev // narrow
    pos_dev = local_len // wide
    seq_total = seq_dev * wide
    sizes = (narrow, wide, experts // narrow)

    wall_own = jnp.concatenate(
        [
            input_projection_weight.reshape(features, -1),
            jnp.transpose(output_projection_weight),
        ],
        axis=1,
    )
    row_pos = lax.dynamic_slice_in_dim(positions, z * own_seqs, own_seqs, 0)
    starts = jnp.arange(length, dtype=jnp.int32)[None, :] - row_pos
    offset_rows = w * pos_dev
    index_rows = lax.dynamic_slice_in_dim(members_index, offset_rows, pos_dev, 0)
    live = lax.dynamic_slice_in_dim(members_mask, offset_rows, pos_dev, 0) > 0
    named = (
        index_rows[..., None] == jnp.arange(seq_total, dtype=jnp.int32)[None, None, None, :]
    ) & live[..., None]
    group_of = jnp.max(
        jnp.where(named, jnp.arange(groups, dtype=jnp.int32)[None, :, None, None], 0), axis=(1, 2)
    )
    key_row = group_of + groups * jnp.arange(pos_dev, dtype=jnp.int32)[:, None]
    key_row = jnp.transpose(key_row).reshape(1, seq_total * pos_dev)

    gain_one, gain_two = gain_attn.reshape(1, features), gain_mixer.reshape(1, features)
    router = jnp.transpose(weight_router)
    x_mix, g_mix, weights, x_seq, wall, qkv, att, lse = forward(
        inputs, cotangent, wall_own, weight_up, weight_down, starts[:, :, None], gain_one, sizes
    )
    outputs, gx, full, g_wall, small = backward(
        x_mix,
        g_mix,
        weights,
        x_seq,
        wall,
        qkv,
        att,
        (key_row, groups),
        starts[:, None, :],
        lse,
        gain_one,
        gain_two,
        router,
        inputs.shape,
        sizes,
    )
    full = full.reshape((2, experts) + full.shape[3:]).astype(f32)
    g_wall = g_wall.astype(f32)
    return (
        outputs,
        gx.astype(f32),
        small[experts + 1],
        g_wall[:, : 3 * PAIR].reshape(input_projection_weight.shape),
        jnp.transpose(g_wall[:, 3 * PAIR :]),
        small[experts],
        jnp.transpose(small[:experts]),
        full[0],
        full[1],
    )


def solution(mesh):
    in_specs = (
        P("wide", "narrow", None),
        P("wide", None),
        P("narrow", None, None),
        P("narrow", None, None),
        P(),
        P(None, None, "narrow"),
        P("narrow", None),
        P(),
        P(),
        P(None, None, "narrow"),
        P(None, "narrow", None),
        P("wide", "narrow", None),
    )
    out_specs = (
        P("wide", "narrow", None),
        P("wide", "narrow", None),
        P(),
        P(None, None, "narrow"),
        P("narrow", None),
        P(),
        P(),
        P(None, None, "narrow"),
        P(None, "narrow", None),
    )
    return jax.shard_map(
        per_device, mesh=mesh, in_specs=in_specs, out_specs=out_specs, check_vma=False
    )
```

time: 1430 us -> 415 us (0.29)
  waiting for transfers between devices: 816 us -> 0 us
  Pallas kernels: 0 us -> 374 us
  matrix products: 298 us -> 0 us
  other arithmetic: 136 us -> 5.99 us
  blocking collectives: 99.7 us -> 0 us
  local copies, waits for them, and re-layouts: 42.3 us -> 25.7 us
    pallas_call x0 -> x2, Pallas kernels: none -> 374 us  [the longest x1 237 us: backward(): pl.pallas_call(functools.partial(backward_body, sizes, min(256, length),...]
    reduce_scatter x4 -> x0, waiting for transfers between devices: 346 us -> none  [the longest x1 142 us: per_device(): lax.psum_scatter(jnp.einsum('pbi,iq->pbq', current_row_block, output_proj...]
    all_gather x4 -> x0, waiting for transfers between devices: 321 us -> none  [the longest x1 143 us: per_device(): lax.all_gather(normed_one.astype(jnp.bfloat16), 'narrow', axis=1, tiled=T...]
    dot_general x36 -> x0, matrix products: 294 us -> none  [the longest x2 45.8 us: per_device(): jnp.einsum('qshd,skhd->shqk', grad_out_block, values_local, preferred_ele...]
    psum x1 -> x0, waiting for transfers between devices: 88.7 us -> none  [per_device(): lax.psum(inproj_grad.astype(jnp.bfloat16), 'wide').astype(jnp.float32)]
    convert_element_type x11 -> x2, other arithmetic: 78.5 us -> 2.71 us  [the longest x1 2.59 us: per_device(): gx.astype(f32)]
    all_to_all x2 -> x0, waiting for transfers between devices: 60.3 us -> none  [the longest x1 35.6 us: per_device(): lax.all_to_all(token_out, 'wide', split_axis=0, concat_axis=1, tiled=True)]
    all_to_all x2 -> x0, blocking collectives: 58.6 us -> none  [the longest x1 29.4 us: per_device(): lax.all_to_all(grad_grouped, 'wide', split_axis=0, concat_axis=1, tiled=T...]
  transfers between devices with their start and end apart: 11 -> 0, of which waited for: 11 -> 0; matrix products, arithmetic and copies ran while one was open for 6% -> 0% of each run, Pallas kernels for 0% -> 0%
where the time goes in v3:
time: 415 us; the launch traced here: 407 us
  Pallas kernels  374 us (90%)
  local copies, waits for them, and re-layouts  25.7 us (6%)
  other arithmetic  5.99 us (1%)
    pallas_call x1, Pallas kernels, backward(): pl.pallas_call(functools.partial(backward_body, sizes, min(256, length),...  237 us
    pallas_call x1, Pallas kernels, forward(): pl.pallas_call(functools.partial(forward_body, sizes, min(256, length), b...  137 us
    slice x1, local copies, waits for them, and re-layouts, per_device(): full[1]  12.1 us

profile of v3, /device:TPU:3, one launch (start us, length us, event | category | flops | bytes accessed | tf_op | source)
XLA Modules:
  0.0 407.1 jit_solution(7993604244347417072)
XLA Ops:
  0.7 0.8 fusion.3
  1.4 0.8 dynamic-slice_subtract_fusion
  2.2 0.6 broadcast_in_dim.27.start_ref
  2.8 0.9 constant_dynamic-slice_fusion
  3.9 0.8 select_reduce_fusion
  4.8 0.1 copy.54
  4.9 0.7 reshape.56.key_ref
  5.6 1.0 copy.48
  6.6 1.2 copy.47
  7.8 0.2 copy.49
  8.0 0.8 pad_maximum_fusion.wall_own_ref
  8.9 1.3 copy.50.start_ref
  10.2 137.1 %shard_map.187 = (bf16[64,32,512]{2,1,0:T(8,128)(2,1)}, bf16[64,32,512]{2,1,0:T(8,128)(2,1)}, bf16[2,4,512,512]{3,2,1,0:T(8,128)(2,1)}, bf16[2,1024,512]{2,1,0:T...) custom-call(bf16[8,256,512]{2,1,0:T(8,128)(2,1)} %inputs_ref.1, ...), custom_call_target="tpu_custom_call" | custom-call | tf_op jit(solution)/shard_map/pallas_call | solution.py:395
  147.3 237.1 %shard_map.188 = (bf16[8,256,512]{2,1,0:T(8,128)(2,1)}, bf16[8,256,512]{2,1,0:T(8,128)(2,1)}, bf16[2,4,2,512,512]{4,3,2,1,0:T(8,128)(2,1)}, bf16[512,512]{1,0:T(8,128)(2,1)}, f32[16,512]{1,0:T(8,128)}) custom-call(bf16[2048,512]{1,0:T(8,128)(2,1)} %bitcast.23, bf16[2048,512]{1,0:T(8,128)(2,1)} %bitcast.24, ...), custom_call_target="tpu_custom_call" | custom-call | tf_op jit(solution)/shard_map/pallas_call | solution.py:980
  384.4 1.4 fusion.2
  385.8 1.3 slice_bitcast_fusion.1
  387.1 1.1 slice.30
  388.3 0.3 copy.55
  388.5 1.1 copy.56
  389.7 0.1 convert_element_type.11
  389.9 0.8 copy.57
  390.7 2.6 convert_element_type.10
  393.3 12.1 %fusion.1 = (f32[1,4,2,512,512]{4,3,2,1,0:T(8,128)}, f32[1,4,2,512,512]{4,3,2,1,0:T(8,128)}) fusion(bf16[2,4,2,512,512]{4,3,2,1,0:T(8,128)(2,1)} %get-tuple-element.34), kind=kLoop, calls=%fused_computation.12 | loop fusion | bytes 33554432 | tf_op jit(solution)/shard_map/slice | solution.py:1115
  405.4 1.3 copy.60
  (13 shorter events, 0.3 us)
Async XLA Ops:
  387.1 2.6 copy-start
  388.5 2.2 copy-start.1
  393.3 12.1 %copy-start.2 = (bf16[8,256,512]{2,1,0:T(8,128)(2,1)S(1)}, bf16[8,256,512]{2,1,0:T(8,128)(2,1)}, u32[]{:S(2)}) copy-start(bf16[8,256,512]{2,1,0:T(8,128)(2,1)} %get-tuple-element.86) | copy-start | bytes 6291460
